TPU v7x, 128 devices: a whole 4x4x4 slice. The times are simulated.
128 devices in a mesh: island: 16 (over y, z_hi, core), fsdp: 8 (over x, z_lo).
Axes of the slice: x: 4, y: 4, z: 4 (z_hi: 2, z_lo: 2; z = z_hi * 2 + z_lo), core: 2. Of those that a mesh axis runs over, the one named last changes fastest.
Arguments:
- tokens: bfloat16 [65536, 2048], P(('island', 'fsdp')), may hold values from -6 to 6
- cotangent: bfloat16 [65536, 2048], P(('island', 'fsdp')), may hold values from -0.09375 to 0.09375
- norm_gain: float32 [16, 2048], P('island'), may hold values from 0.5 to 1.5
- qkv_weight: bfloat16 [16, 2048, 1536], P('island', 'fsdp'), may hold values from -0.125 to 0.125
- out_weight: bfloat16 [16, 1024, 2048], P('island', 'fsdp'), may hold values from -0.1875 to 0.1875
- gain_first: float32 [16, 2048], P('island'), may hold values from -2 to 2
- gain_second: float32 [16, 2048], P('island'), may hold values from 0.01 to 1
- qkv_first: float32 [16, 2048, 1536], P('island', 'fsdp'), may hold values from -2 to 2
- qkv_second: float32 [16, 2048, 1536], P('island', 'fsdp'), may hold values from 0.01 to 1
- out_first: float32 [16, 1024, 2048], P('island', 'fsdp'), may hold values from -2 to 2
- out_second: float32 [16, 1024, 2048], P('island', 'fsdp'), may hold values from 0.01 to 1
- gain_global: float32 [2048], replicated, may hold values from 0.5 to 1.5
- gain_momentum: float32 [2048], replicated, may hold values from -1 to 1
- qkv_global: float32 [2048, 1536], P('fsdp', 'island'), may hold values from -0.125 to 0.125
- qkv_momentum: float32 [2048, 1536], P('fsdp', 'island'), may hold values from -0.1 to 0.1
- out_global: float32 [1024, 2048], P('fsdp', 'island'), may hold values from -0.1875 to 0.1875
- out_momentum: float32 [1024, 2048], P('fsdp', 'island'), may hold values from -0.1 to 0.1
Outputs:
- gain_next: float32 [16, 2048], P('island')
- qkv_next: bfloat16 [16, 2048, 1536], P('island', 'fsdp')
- out_next: bfloat16 [16, 1024, 2048], P('island', 'fsdp')
- gain_first_next: float32 [16, 2048], P('island')
- gain_second_next: float32 [16, 2048], P('island')
- qkv_first_next: float32 [16, 2048, 1536], P('island', 'fsdp')
- qkv_second_next: float32 [16, 2048, 1536], P('island', 'fsdp')
- out_first_next: float32 [16, 1024, 2048], P('island', 'fsdp')
- out_second_next: float32 [16, 1024, 2048], P('island', 'fsdp')
- gain_global_next: float32 [2048], replicated
- gain_momentum_next: float32 [2048], replicated
- qkv_global_next: float32 [2048, 1536], P('fsdp', 'island')
- qkv_momentum_next: float32 [2048, 1536], P('fsdp', 'island')
- out_global_next: float32 [1024, 2048], P('fsdp', 'island')
- out_momentum_next: float32 [1024, 2048], P('fsdp', 'island')
All inputs are finite; a program needn't handle non-finite values.
Results may differ from a plain program's by a relative error of at most 0.01.
Values may be sent and summed in bfloat16 or wider, within the bound.
A program may use at most 192 MiB of HBM per device.

v0:
```python
import jax
import jax.numpy as jnp
from jax import lax
from jax.sharding import PartitionSpec as P

HEADS = 16
KV_HEADS = 4
HEAD_DIM = 64


BETA_ONE = 0.9
BETA_TWO = 0.95
ADAM_EPS = 1e-08
INNER_RATE = 0.001
WEIGHT_DECAY = 0.1
STEP_COUNT = 100.0
OUTER_RATE = 0.7
OUTER_MOMENTUM = 0.9
MIXING = 0.5
NORM_EPS = 1e-05
ROPE_BASE = 500000.0


def rotary(heads, positions):
    half = heads.shape[-1] // 2
    freqs = ROPE_BASE ** (-jnp.arange(half, dtype=jnp.float32) / half)
    angles = positions[:, None] * freqs[None, :]
    cosine = jnp.cos(angles)[:, None, :]
    sine = jnp.sin(angles)[:, None, :]
    first = heads[..., :half]
    second = heads[..., half:]
    return jnp.concatenate(
        [first * cosine - second * sine, first * sine + second * cosine], axis=-1
    )


def attend_part(seq, gain, wqkv):
    length = seq.shape[0]
    wide = seq.astype(jnp.float32)
    factor = lax.rsqrt(jnp.mean(wide * wide, axis=-1, keepdims=True) + NORM_EPS)
    normed = (wide * factor * gain).astype(jnp.bfloat16)
    mixed = jnp.dot(normed, wqkv, preferred_element_type=jnp.float32)
    qwidth = HEADS * HEAD_DIM
    kwidth = KV_HEADS * HEAD_DIM
    queries = mixed[:, :qwidth].reshape(length, HEADS, HEAD_DIM)
    keys = mixed[:, qwidth : qwidth + kwidth].reshape(length, KV_HEADS, HEAD_DIM)
    values = mixed[:, qwidth + kwidth :].reshape(length, KV_HEADS, HEAD_DIM).astype(jnp.bfloat16)
    positions = jnp.arange(length, dtype=jnp.float32)
    queries = rotary(queries, positions).astype(jnp.bfloat16)
    keys = rotary(keys, positions).astype(jnp.bfloat16)
    queries = queries.reshape(length, KV_HEADS, HEADS // KV_HEADS, HEAD_DIM)
    scores = jnp.einsum(
        "qkgd,skd->kgqs", queries, keys, preferred_element_type=jnp.float32
    ) * HEAD_DIM ** (-0.5)
    causal = positions[:, None] >= positions[None, :]
    scores = jnp.where(causal, scores, -1e30)
    weights = jax.nn.softmax(scores, axis=-1).astype(jnp.bfloat16)
    attended = jnp.einsum("kgqs,skd->qkgd", weights, values, preferred_element_type=jnp.float32)
    return attended.astype(jnp.bfloat16).reshape(length, qwidth)


def project_out(attended, wout):
    return jnp.dot(attended, wout, preferred_element_type=jnp.float32)


def sequence_grads(seq, cot, gain, wqkv, wout):

    def loss(gain_in, qkv_in, out_in):
        return jnp.sum(
            project_out(attend_part(seq, gain_in, qkv_in), out_in) * cot.astype(jnp.float32)
        )

    return jax.grad(loss, argnums=(0, 1, 2))(gain, wqkv, wout)


def adamw(param, grad, first, second, decay):
    wide = param.astype(jnp.float32)
    first_next = BETA_ONE * first + (1.0 - BETA_ONE) * grad
    second_next = BETA_TWO * second + (1.0 - BETA_TWO) * grad * grad
    update = (
        first_next
        / (1.0 - BETA_ONE**STEP_COUNT)
        / (jnp.sqrt(second_next / (1.0 - BETA_TWO**STEP_COUNT)) + ADAM_EPS)
    )
    return (wide - INNER_RATE * (update + decay * wide), first_next, second_next)


def nesterov(global_value, momentum, average):
    delta = global_value - average
    momentum_next = OUTER_MOMENTUM * momentum + delta
    return (global_value - OUTER_RATE * (delta + OUTER_MOMENTUM * momentum_next), momentum_next)


def inner_step(tokens, cotangent, gain, local_qkv, local_out, moments):
    full_qkv, full_out = (
        lax.all_gather(local_qkv, "fsdp", axis=0, tiled=True),
        lax.all_gather(local_out, "fsdp", axis=0, tiled=True),
    )
    g_gain, g_qkv, g_out = sequence_grads(tokens, cotangent, gain, full_qkv, full_out)
    sum_qkv, sum_out = (
        lax.psum_scatter(
            g_qkv.astype(jnp.float32).astype(jnp.bfloat16), "fsdp", scatter_dimension=0, tiled=True
        ).astype(jnp.float32),
        lax.psum_scatter(
            g_out.astype(jnp.float32).astype(jnp.bfloat16), "fsdp", scatter_dimension=0, tiled=True
        ).astype(jnp.float32),
    )
    sum_gain = lax.psum(g_gain, "fsdp")
    gain_state = adamw(gain, sum_gain, moments[0], moments[1], 0.0)
    qkv_state = adamw(local_qkv, sum_qkv, moments[2], moments[3], WEIGHT_DECAY)
    out_state = adamw(local_out, sum_out, moments[4], moments[5], WEIGHT_DECAY)
    return (gain_state, qkv_state, out_state)


def outer_sync(gain, local_qkv, local_out, outer_state):
    islands = lax.axis_size("island")
    scale = 1.0 / islands
    qkv_total, out_total = (
        lax.psum_scatter(
            local_qkv.astype(jnp.float32).astype(jnp.bfloat16),
            "island",
            scatter_dimension=1,
            tiled=True,
        ).astype(jnp.float32),
        lax.psum_scatter(
            local_out.astype(jnp.float32).astype(jnp.bfloat16),
            "island",
            scatter_dimension=1,
            tiled=True,
        ).astype(jnp.float32),
    )
    gain_total = lax.psum(gain, "island")
    gain_global, gain_momentum, qkv_global, qkv_momentum, out_global, out_momentum = outer_state
    gain_pair = nesterov(gain_global, gain_momentum, gain_total * scale)
    qkv_pair = nesterov(qkv_global, qkv_momentum, qkv_total * scale)
    out_pair = nesterov(out_global, out_momentum, out_total * scale)
    qkv_whole, out_whole = (
        lax.all_gather(qkv_pair[0].astype(jnp.bfloat16), "island", axis=1, tiled=True).astype(
            jnp.float32
        ),
        lax.all_gather(out_pair[0].astype(jnp.bfloat16), "island", axis=1, tiled=True).astype(
            jnp.float32
        ),
    )
    return (gain_pair, qkv_pair, out_pair, qkv_whole, out_whole)


def shards(
    tokens,
    cotangent,
    norm_gain,
    qkv_weight,
    out_weight,
    gain_first,
    gain_second,
    qkv_first,
    qkv_second,
    out_first,
    out_second,
    gain_global,
    gain_momentum,
    qkv_global,
    qkv_momentum,
    out_global,
    out_momentum,
):
    gain = norm_gain[0]
    local_qkv = qkv_weight[0]
    local_out = out_weight[0]
    moments = (
        gain_first[0],
        gain_second[0],
        qkv_first[0],
        qkv_second[0],
        out_first[0],
        out_second[0],
    )
    outer_state = (gain_global, gain_momentum, qkv_global, qkv_momentum, out_global, out_momentum)
    stepped = inner_step(tokens, cotangent, gain, local_qkv, local_out, moments)
    synced = outer_sync(gain, local_qkv, local_out, outer_state)
    gain_state, qkv_state, out_state = stepped
    gain_pair, qkv_pair, out_pair, qkv_whole, out_whole = synced
    gain_next = MIXING * gain_state[0] + (1.0 - MIXING) * gain_pair[0]
    qkv_next = (MIXING * qkv_state[0] + (1.0 - MIXING) * qkv_whole).astype(jnp.bfloat16)
    out_next = (MIXING * out_state[0] + (1.0 - MIXING) * out_whole).astype(jnp.bfloat16)
    return (
        gain_next[None],
        qkv_next[None],
        out_next[None],
        gain_state[1][None],
        gain_state[2][None],
        qkv_state[1][None],
        qkv_state[2][None],
        out_state[1][None],
        out_state[2][None],
        gain_pair[0],
        gain_pair[1],
        qkv_pair[0],
        qkv_pair[1],
        out_pair[0],
        out_pair[1],
    )


def solution(mesh):
    placed = (
        P(("island", "fsdp"), None),
        P(("island", "fsdp"), None),
        P("island", None),
        P("island", "fsdp", None),
        P("island", "fsdp", None),
        P("island", None),
        P("island", None),
        P("island", "fsdp", None),
        P("island", "fsdp", None),
        P("island", "fsdp", None),
        P("island", "fsdp", None),
        P(),
        P(),
        P("fsdp", "island"),
        P("fsdp", "island"),
        P("fsdp", "island"),
        P("fsdp", "island"),
    )
    return jax.shard_map(
        shards,
        mesh=mesh,
        in_specs=placed,
        out_specs=(
            P("island", None),
            P("island", "fsdp", None),
            P("island", "fsdp", None),
            P("island", None),
            P("island", None),
            P("island", "fsdp", None),
            P("island", "fsdp", None),
            P("island", "fsdp", None),
            P("island", "fsdp", None),
            P(),
            P(),
            P("fsdp", "island"),
            P("fsdp", "island"),
            P("fsdp", "island"),
            P("fsdp", "island"),
        ),
        check_vma=False,
    )
```

profile of v0, /device:TPU:64, one launch (start us, length us, event | category | flops | bytes accessed | tf_op | source)
XLA Modules:
  0.0 552.8 jit_solution(3314176061706514818)
XLA Ops:
  9.6 2.0 copy.83
  11.7 2.3 copy.81
  14.3 2.1 fusion.17
  16.7 86.8 %all-gather.5.cloned.1.call-done = bf16[1,1024,2048]{2,1,0:T(8,128)(2,1)} async-done(((bf16[1,128,2048]{2,1,0:T(8,128)(2,1)}), bf16[1,1024,2048]{2,1,0:T(8,128)(2,1)}) %all-gather.5.cloned.1.call-update) | async-done | bytes 4194320 | tf_op jit(solution)/shard_map/all_gather | solution.py:97
  103.5 5.5 fusion.33
  109.0 1.5 copy.62
  110.5 127.5 %all-gather.7.cloned.1.call-done = bf16[1,2048,1536]{2,1,0:T(8,128)(2,1)} async-done(((bf16[1,256,1536]{2,1,0:T(8,128)(2,1)}), bf16[1,2048,1536]{2,1,0:T(8,128)(2,1)}) %all-gather.7.cloned.1.call-update) | async-done | bytes 6291472 | tf_op jit(solution)/shard_map/all_gather | solution.py:96
  238.1 6.3 %fusion.11 = f32[512,1536]{1,0:T(8,128)S(1)} fusion(bf16[1,2048,1536]{2,1,0:T(8,128)(2,1)} %all-gather.7.cloned.1.call-done, bf16[512,2048]{1,0:T(8,128)(2,1)} %param.17, f32[2048]{0:T(1024)S(1)} %bitcast.185, f32[512]{0:T(512)S(1)} %add_rsqrt_fusion), kind=kOutput, calls=%fused_computation.18 | convolution fusion | flops 3225419776 | bytes 11544576 | tf_op jit(solution)/shard_map/jvp()/dot_general | solution.py:42
  244.4 1.5 slice.32
  247.5 2.9 copy.64
  250.3 2.0 copy.63
  252.4 1.9 subtract_convert_fusion
  255.8 7.8 %fusion.7 = (f32[4,4,512]{2,1,0:T(4,128)}, f32[4,512,512,4]{2,1,3,0:T(8,128)}) fusion(pred[512,512]{0,1:T(8,128)(4,1)S(1)} %iota_compare_fusion.1, bf16[512,4,4,32]{0,3,2,1:T(8,128)(2,1)S(1)} %bitcast.169, bf16[512,4,4,32]{0,3,2,1:T(8,128)(2,1)S(1)} %bitcast.167, bf16[512,4,32]{0,2,1:T(8,128)(2,1)S(1)} %get-tuple-element.85, ...), kind=kOutput, calls=%fused_computation.12 | convolution fusion | flops 552067072 | bytes 18382848 | tf_op jit(solution)/shard_map/jvp(qkgd,skd->kgqs)/dot_general | solution.py:52
  263.6 9.8 %fusion.8 = f32[4,4,512]{2,1,0:T(4,128)} fusion(f32[4,512,512,4]{2,1,3,0:T(8,128)} %get-tuple-element.90, f32[4,4,512]{2,1,0:T(4,128)} %get-tuple-element.89, pred[512,512]{0,1:T(8,128)(4,1)S(1)} %iota_compare_fusion.1), kind=kLoop, calls=%fused_computation.13 | loop fusion | flops 16769024 | bytes 17104896 | tf_op jit(solution)/shard_map/jvp()/reduce_sum | solution.py:57
  274.8 1.8 copy.66
  276.6 16.6 %divide_convert_fusion = (bf16[4,4,512,512]{2,3,1,0:T(8,128)(2,1)}, f32[4,4,512]{2,1,0:T(4,128)}, bf16[4,4,512,512]{2,3,1,0:T(8,128)(2,1)}) fusion(f32[4,512,512,4]{2,1,3,0:T(8,128)} %get-tuple-element.90, f32[4,4,512]{2,1,0:T(4,128)} %fusion.8, f32[4,4,512]{2,1,0:T(4,128)} %get-tuple-element.89, pred[512,512]{0,1:T(8,128)(4,1)S(1)} %iota_compare_fusion.1, ...), kind=kOutput, calls=%fused_computation.10 | convolution fusion | flops 578805760 | bytes 35258368 | tf_op jit(solution)/shard_map/transpose(jvp(kgqs,skd->qkgd))/dot_general | solution.py:58
  293.2 4.9 convolution_convert_fusion.3
  298.2 4.3 convolution_convert_fusion.2
  303.3 11.3 %fusion.4 = bf16[4,512,512,4]{2,1,3,0:T(8,128)(2,1)S(1)} fusion(bf16[4,4,512,512]{2,3,1,0:T(8,128)(2,1)} %get-tuple-element.91, f32[4,512,512,4]{2,1,3,0:T(8,128)} %get-tuple-element.90, f32[4,512,4]{1,2,0:T(4,128)S(1)} %bitcast.183, f32[4,512,4]{1,2,0:T(4,128)S(1)} %negate_bitcast_fusion, f32[4,512,4]{1,2,0:T(4,128)S(1)} %bitcast.180, ...), kind=kLoop, calls=%fused_computation.6 | loop fusion | flops 41943040 | bytes 33914880 | tf_op jit(solution)/shard_map/transpose(jvp())/mul | solution.py:52
  314.6 2.6 fusion.40
  318.2 3.0 fusion.32
  321.2 2.0 multiply_add_fusion.1
  323.4 2.7 fusion.41
  326.8 6.9 %convolution_convert_fusion = bf16[2048,1536]{1,0:T(8,128)(2,1)} fusion(f32[512,1024]{0,1:T(8,128)S(1)} %bitcast.172, f32[512,256]{0,1:T(8,128)S(1)} %bitcast.179, bf16[512,256]{0,1:T(8,128)(2,1)S(1)} %bitcast.181, bf16[512,2048]{1,0:T(8,128)(2,1)S(1)} %copy-done.9, f32[2048]{0:T(1024)S(1)} %bitcast.186, f32[512]{0:T(512)S(1)} %add_rsqrt_fusion), kind=kOutput, calls=%fused_computation.14 | convolution fusion | flops 3230924800 | bytes 11282432 | tf_op jit(solution)/shard_map/transpose(jvp())/dot_general | solution.py:42
  334.7 34.7 %psum.15 = f32[2048]{0:T(1024)S(1)} all-reduce(f32[2048]{0:T(1024)S(1)} %bitcast.187), channel_id=1, replica_groups=mesh['island'=16,'fsdp'=8] {'island'}, use_global_device_ids=true, to_apply=%region_6.7 | all-reduce | flops 2048 | bytes 16384 | tf_op jit(solution)/shard_map/psum | solution.py:132
  371.1 32.8 %all_gather.15 = bf16[128,2048]{1,0:T(8,128)(2,1)} all-gather(bf16[128,128]{1,0:T(8,128)(2,1)S(1)} %get-tuple-element.60), channel_id=1, replica_groups=mesh['island'=16,'fsdp'=8] {'island'}, dimensions={1}, use_global_device_ids=true | all-gather | bytes 557056 | tf_op jit(solution)/shard_map/all_gather | solution.py:141
  405.0 39.3 %all_gather.14 = bf16[256,1536]{0,1:T(8,128)(2,1)S(1)} all-gather(bf16[256,96]{0,1:T(8,128)(2,1)S(1)} %copy.70), channel_id=1, replica_groups=mesh['island'=16,'fsdp'=8] {'island'}, dimensions={1}, use_global_device_ids=true | all-gather | bytes 835584 | tf_op jit(solution)/shard_map/all_gather | solution.py:138
  446.9 8.2 %fusion.16 = f32[2048]{0:T(1024)S(1)} fusion(bf16[512,2048]{1,0:T(8,128)(2,1)} %param.17, f32[512]{0:T(512)S(1)} %add_rsqrt_fusion, bf16[1,2048,1536]{2,1,0:T(8,128)(2,1)} %all-gather.7.cloned.1.call-done, f32[512,1024]{0,1:T(8,128)} %bitcast.173, f32[512,256]{0,1:T(8,128)} %bitcast.178, bf16[512,256]{0,1:T(8,128)(2,1)} %bitcast.182), kind=kOutput, calls=%fused_computation.25 | convolution fusion | flops 3229874176 | bytes 11282432 | tf_op jit(solution)/shard_map/transpose(jvp())/dot_general | solution.py:42
  455.2 18.7 %psum.14 = f32[2048]{0:T(1024)S(1)} all-reduce(f32[2048]{0:T(1024)S(1)} %fusion.16), channel_id=1, replica_groups=mesh['island'=16,'fsdp'=8] {'fsdp'}, use_global_device_ids=true, to_apply=%region_5.6 | all-reduce | flops 2048 | bytes 16384 | tf_op jit(solution)/shard_map/psum | solution.py:108
  474.5 4.3 fusion.56
  478.8 60.7 %reduce-scatter.9.cloned.1.call-done = bf16[256,1536]{1,0:T(8,128)(2,1)} async-done(((bf16[2048,1536]{1,0:T(8,128)(2,1)}), bf16[256,1536]{1,0:T(8,128)(2,1)}) %reduce-scatter.9.cloned.1.call-update) | async-done | bytes 786448 | tf_op jit(solution)/shard_map/reduce_scatter | solution.py:101
  539.5 5.7 %fusion.50 = (f32[1,256,1536]{2,1,0:T(8,128)}, bf16[1,256,1536]{2,1,0:T(8,128)(2,1)}, f32[1,256,1536]{2,1,0:T(8,128)}) fusion(bf16[256,1536]{1,0:T(8,128)(2,1)} %reduce-scatter.9.cloned.1.call-done, f32[1,256,1536]{2,1,0:T(8,128)} %param.25, bf16[256,1536]{1,0:T(8,128)(2,1)} %copy.71, f32[1,256,1536]{2,1,0:T(8,128)} %param.24, ...), kind=kLoop, calls=%fused_computation.75 | loop fusion | flops 8257536 | bytes 9437184 | tf_op jit(solution)/shard_map/broadcast_in_dim | solution.py:193
  (106 shorter events, 16.2 us)
Async XLA Ops:
  8.0 95.5 %copy-start = (bf16[512,2048]{1,0:T(8,128)(2,1)S(1)}, bf16[512,2048]{1,0:T(8,128)(2,1)}, u32[]{:S(2)}) copy-start(bf16[512,2048]{1,0:T(8,128)(2,1)} %param.18) | copy-start | bytes 6291460
  8.0 95.5 %all-gather.5.cloned.1.call-start = ((), (), s32[]{:S(2)}) async-start(), calls=%async_computation.6 | async-start | bytes 4718592 | tf_op jit(solution)/shard_map/all_gather | solution.py:97
  8.8 229.3 %all-gather.7.cloned.1.call-start = ((), (), s32[]{:S(2)}) async-start(), calls=%async_computation.7 | async-start | bytes 7077888 | tf_op jit(solution)/shard_map/all_gather | solution.py:96
  9.5 360.0 %reduce-scatter.15.cloned.1.call-start = ((), (), s32[]{:S(2)}) async-start(), calls=%async_computation.9 | async-start | bytes 557056
  11.6 392.3 %reduce-scatter.13.cloned.1.call-start = ((), (), s32[]{:S(2)}) async-start(), calls=%async_computation.8 | async-start | bytes 835584
  14.0 460.5 %reduce-scatter.11.cloned.1.call-start = ((), (), s32[]{:S(2)}) async-start(), calls=%async_computation.5 | async-start | bytes 4718592 | tf_op jit(solution)/shard_map/reduce_scatter | solution.py:104
  16.7 221.4 %copy-start.24 = (f32[1,2048]{1,0:T(1,128)S(1)}, f32[1,2048]{1,0:T(1,128)}, u32[]{:S(2)}) copy-start(f32[1,2048]{1,0:T(1,128)} %param.19) | copy-start | bytes 24580
  110.5 166.1 %copy-start.3 = (bf16[512,1024]{0,1:T(8,128)(2,1)}, bf16[512,1024]{0,1:T(8,128)(2,1)S(1)}, u32[]{:S(2)}) copy-start(bf16[512,1024]{0,1:T(8,128)(2,1)S(1)} %copy.62) | copy-start | bytes 3145732
  254.3 9.3 %copy-start.5 = (bf16[512,16,32]{0,2,1:T(8,128)(2,1)}, bf16[512,16,32]{0,2,1:T(8,128)(2,1)S(1)}, u32[]{:S(2)}) copy-start(bf16[512,16,32]{0,2,1:T(8,128)(2,1)S(1)} %get-tuple-element.77) | copy-start | bytes 1572868
  254.3 9.3 %copy-start.7 = (bf16[512,16,32]{0,2,1:T(8,128)(2,1)}, bf16[512,16,32]{0,2,1:T(8,128)(2,1)S(1)}, u32[]{:S(2)}) copy-start(bf16[512,16,32]{0,2,1:T(8,128)(2,1)S(1)} %get-tuple-element.78) | copy-start | bytes 1572868
  255.8 7.8 %copy-start.12 = (bf16[512,4,32]{0,2,1:T(8,128)(2,1)}, bf16[512,4,32]{0,2,1:T(8,128)(2,1)S(1)}, u32[]{:S(2)}) copy-start(bf16[512,4,32]{0,2,1:T(8,128)(2,1)S(1)} %get-tuple-element.84) | copy-start | bytes 393220
  255.8 7.8 %copy-start.14 = (bf16[512,4,32]{0,2,1:T(8,128)(2,1)}, bf16[512,4,32]{0,2,1:T(8,128)(2,1)S(1)}, u32[]{:S(2)}) copy-start(bf16[512,4,32]{0,2,1:T(8,128)(2,1)S(1)} %get-tuple-element.85) | copy-start | bytes 393220
  276.6 16.6 %copy-start.11 = (bf16[512,256]{0,1:T(8,128)(2,1)S(1)}, bf16[512,256]{0,1:T(8,128)(2,1)}, u32[]{:S(2)}) copy-start(bf16[512,256]{0,1:T(8,128)(2,1)} %copy.66) | copy-start | bytes 786436
  302.5 237.0 %reduce-scatter.9.cloned.1.call-start = ((), (), s32[]{:S(2)}) async-start(), calls=%async_computation.4 | async-start | bytes 7077888 | tf_op jit(solution)/shard_map/reduce_scatter | solution.py:101
  303.3 11.3 %copy-start.6 = (bf16[512,16,32]{0,2,1:T(8,128)(2,1)S(1)}, bf16[512,16,32]{0,2,1:T(8,128)(2,1)}, u32[]{:S(2)}) copy-start(bf16[512,16,32]{0,2,1:T(8,128)(2,1)} %copy-done.5) | copy-start | bytes 1572868
  303.3 11.3 %copy-start.8 = (bf16[512,16,32]{0,2,1:T(8,128)(2,1)S(1)}, bf16[512,16,32]{0,2,1:T(8,128)(2,1)}, u32[]{:S(2)}) copy-start(bf16[512,16,32]{0,2,1:T(8,128)(2,1)} %copy-done.7) | copy-start | bytes 1572868
  314.6 3.6 copy-start.13
  314.6 3.6 copy-start.15
  317.4 6.0 %slice-start = ((s8[8388608]{0:T(1024)(128)(4,1)}), s8[4194304]{0:T(1024)(128)(4,1)S(1)}, s32[]{:S(2)}) async-start(s8[8388608]{0:T(1024)(128)(4,1)} %bitcast.158), calls=%async_computation.10 | async-start | bytes 8388608
  318.2 5.2 slice-start.1
  321.2 2.2 copy-start.4
  323.4 2.7 copy-start.10
  323.4 3.4 copy-start.9
  323.4 3.4 copy-start.16
  333.7 35.8 %copy-start.28 = (f32[1,2048]{1,0:T(1,128)S(1)}, f32[1,2048]{1,0:T(1,128)}, u32[]{:S(2)}) copy-start(f32[1,2048]{1,0:T(1,128)} %param.22) | copy-start | bytes 24580
  333.7 35.8 %copy-start.29 = (f32[1,2048]{1,0:T(1,128)S(1)}, f32[1,2048]{1,0:T(1,128)}, u32[]{:S(2)}) copy-start(f32[1,2048]{1,0:T(1,128)} %param.23) | copy-start | bytes 24580
  333.7 36.7 %copy-start.22 = (f32[128,128]{1,0:T(8,128)S(1)}, f32[128,128]{1,0:T(8,128)}, u32[]{:S(2)}) copy-start(f32[128,128]{1,0:T(8,128)} %param.32) | copy-start | bytes 196612
  333.7 36.7 %copy-start.23 = (f32[128,128]{1,0:T(8,128)S(1)}, f32[128,128]{1,0:T(8,128)}, u32[]{:S(2)}) copy-start(f32[128,128]{1,0:T(8,128)} %param.33) | copy-start | bytes 196612
  446.9 26.9 %copy-start.26 = (f32[2048]{0:T(1024)S(1)}, f32[2048]{0:T(1024)}, u32[]{:S(2)}) copy-start(f32[2048]{0:T(1024)} %param.28) | copy-start | bytes 24580
  446.9 26.9 %copy-start.27 = (f32[2048]{0:T(1024)S(1)}, f32[2048]{0:T(1024)}, u32[]{:S(2)}) copy-start(f32[2048]{0:T(1024)} %param.29) | copy-start | bytes 24580
  446.9 27.6 %copy-start.2 = (bf16[1,128,2048]{2,1,0:T(8,128)(2,1)S(1)}, bf16[1,128,2048]{2,1,0:T(8,128)(2,1)}, u32[]{:S(2)}) copy-start(bf16[1,128,2048]{2,1,0:T(8,128)(2,1)} %param.21) | copy-start | bytes 1572868
  455.2 84.4 %copy-start.1 = (bf16[1,256,1536]{2,1,0:T(8,128)(2,1)S(1)}, bf16[1,256,1536]{2,1,0:T(8,128)(2,1)}, u32[]{:S(2)}) copy-start(bf16[1,256,1536]{2,1,0:T(8,128)(2,1)} %param.20) | copy-start | bytes 2359300
  (6 other events, 4.9 us)
Sparse Core Ops, SparseCore 0:
  10.5 92.9 all-gather.4
  105.1 132.8 all-gather.6
Sparse Core Ops, SparseCore 1:
  14.3 79.9 reduce-scatter.14
  99.0 106.6 reduce-scatter.12
  302.6 97.4 reduce-scatter.10
  402.6 136.8 reduce-scatter.8
where the time goes:
time: 555 us; the launch traced here: 553 us
  waiting for transfers between devices  277 us (50%)
  blocking collectives  125 us (23%)
  matrix products  68.9 us (12%)
  other arithmetic  43.1 us (8%)
  local copies, waits for them, and re-layouts  22.4 us (4%)
  between operations  16.2 us (3%)
    all_gather x1, waiting for transfers between devices, inner_step(): lax.all_gather(local_qkv, 'fsdp', axis=0, tiled=True)  128 us
    all_gather x1, waiting for transfers between devices, inner_step(): lax.all_gather(local_out, 'fsdp', axis=0, tiled=True)  86.8 us
    reduce_scatter x1, waiting for transfers between devices, inner_step(): lax.psum_scatter(g_qkv.astype(jnp.float32).astype(jnp.bfloat16), 'fsdp',...  60.7 us
    all_gather x1, blocking collectives, outer_sync(): lax.all_gather(qkv_pair[0].astype(jnp.bfloat16), 'island', axis=1, tiled=...  39.3 us
    psum x1, blocking collectives, outer_sync(): gain_total = lax.psum(gain, 'island')  34.7 us
    all_gather x1, blocking collectives, outer_sync(): lax.all_gather(out_pair[0].astype(jnp.bfloat16), 'island', axis=1, tiled=...  32.8 us
    dot_general x3, matrix products, attend_part(): jnp.einsum('kgqs,skd->qkgd', weights, values, preferred_element_type=jnp....  24.2 us
    dot_general x3, matrix products, attend_part(): mixed = jnp.dot(normed, wqkv, preferred_element_type=jnp.float32)  21.4 us
  transfers between devices with their start and end apart: 6, of which 3 were waited for; matrix products, arithmetic and copies ran while one was open for 23% of the time, Pallas kernels for 0%

commit v1 on v0

v1 whole, which is shorter than its diff:
```python
import functools

import jax
import jax.numpy as jnp
import numpy as np
from jax import lax
from jax.experimental import pallas as pl
from jax.experimental.pallas import tpu as pltpu
from jax.sharding import PartitionSpec as P

HEADS = 16
KV_HEADS = 4
HEAD_DIM = 64
GROUP = HEADS // KV_HEADS

BETA_ONE = 0.9
BETA_TWO = 0.95
ADAM_EPS = 1e-08
INNER_RATE = 0.001
WEIGHT_DECAY = 0.1
STEP_COUNT = 100.0
OUTER_RATE = 0.7
OUTER_MOMENTUM = 0.9
MIXING = 0.5
NORM_EPS = 1e-05
ROPE_BASE = 500000.0

MESH = pl.DeviceIdType.MESH
F32 = jnp.float32
BF16 = jnp.bfloat16

TOK = 512
D = 2048
QW = HEADS * HEAD_DIM
QKV = QW + 2 * KV_HEADS * HEAD_DIM
QROWS = 256
OROWS = 128
HALF = OROWS // 2
COLS = 256
CHUNKS = QKV // COLS
KCHUNK, VCHUNK = QW // COLS, QW // COLS + 1
QB = 256
NT = (((1,), (1,)), ((), ()))


def rope_tables():
    half = HEAD_DIM // 2
    freqs = ROPE_BASE ** (-np.arange(half, dtype=np.float64) / half)
    angles = freqs[:, None] * np.arange(TOK, dtype=np.float64)[None, :]
    return np.cos(angles).astype(np.float32), np.sin(angles).astype(np.float32)


def adamw(param, grad, first, second, decay):
    wide = param.astype(F32)
    first_next = BETA_ONE * first + (1.0 - BETA_ONE) * grad
    second_next = BETA_TWO * second + (1.0 - BETA_TWO) * grad * grad
    update = (
        first_next
        / (1.0 - BETA_ONE**STEP_COUNT)
        / (jnp.sqrt(second_next / (1.0 - BETA_TWO**STEP_COUNT)) + ADAM_EPS)
    )
    return (wide - INNER_RATE * (update + decay * wide), first_next, second_next)


def nesterov(global_value, momentum, average):
    delta = global_value - average
    momentum_next = OUTER_MOMENTUM * momentum + delta
    return (global_value - OUTER_RATE * (delta + OUTER_MOMENTUM * momentum_next), momentum_next)


def rows_of(index, size):
    return pl.ds(pl.multiple_of(index * size, size), size)


def grads_kernel(
    islands,
    x_ref, cot_ref, gain_ref, wq_ref, wo_ref, cos_ref, sin_ref, qglob_ref, qmom_ref, oglob_ref, omom_ref,
    sumq_ref, sumo_ref, sumg_ref, totq_ref, toto_ref, totg_ref, wholeq_ref, wholeo_ref,
    wq, wo, nrm, nrm_t, fac, qkv_t, k_tok, v_tok, datt_t, att_t, dm_t, dm, dk_acc, dv_acc,
    gq, go, rq, ro, ro_z, g_rows, g_recv,
    i_send, i_recv, io_recv, ig_recv, i_back, io_back, i_new, io_new,
    own_sem, agq_s, agq_r, ago_s, ago_r, rsq_s, rsq_r, rso_s, rso_r, gg_s, gg_r, is_s, is_r, ib_s, ib_r,
):
    f = lax.axis_index("fsdp")
    me = lax.axis_index("island")
    a, b = f // 2, f % 2
    qshare = QKV // islands
    oshare = D // islands

    def at_x(step):
        return lax.rem(a + step, 4)

    right = {"fsdp": at_x(1) * 2 + b}
    left = {"fsdp": at_x(3) * 2 + b}
    across = {"fsdp": a * 2 + 1 - b}
    sent = []

    def send(src, dst, s_sem, r_sem, to):
        copy = pltpu.make_async_remote_copy(
            src_ref=src, dst_ref=dst, send_sem=s_sem, recv_sem=r_sem, device_id=to, device_id_type=MESH
        )
        copy.start()
        sent.append((src, s_sem))

    def got(dst, r_sem):
        pltpu.make_async_remote_copy(
            src_ref=dst, dst_ref=dst, send_sem=r_sem, recv_sem=r_sem, device_id=across, device_id_type=MESH
        ).wait_recv()

    def left_here(src, s_sem):
        pltpu.make_async_remote_copy(
            src_ref=src, dst_ref=src, send_sem=s_sem, recv_sem=s_sem, device_id=across, device_id_type=MESH
        ).wait_send()

    barrier = pltpu.get_barrier_semaphore()

    @pl.loop(1, 8)
    def _(step):
        pl.semaphore_signal(barrier, inc=1, device_id={"fsdp": lax.rem(f + step, 8)}, device_id_type=MESH)

    @pl.loop(1, islands)
    def _(step):
        pl.semaphore_signal(
            barrier, inc=1, device_id={"island": lax.rem(me + step, islands)}, device_id_type=MESH
        )

    for i in range(islands):
        i_send[i] = wq_ref[:, i * qshare : (i + 1) * qshare]
    pl.semaphore_wait(barrier, 7 + islands - 1)

    def wq_block(x_at, z_at, c):
        return wq.at[rows_of(x_at * 2 + z_at, QROWS), pl.ds(c * COLS, COLS)]

    def own_chunk(c):
        src = wq_ref.at[:, pl.ds(c * COLS, COLS)]
        dst = wq_block(a, b, c)
        send(src, dst, agq_s.at[c, 0], agq_r.at[c, 0], across)
        send(src, dst, agq_s.at[c, 1], agq_r.at[c, 1 + b], right)
        send(src, dst, agq_s.at[c, 2], agq_r.at[c, 3 + b], left)

    def pair_chunk(c):
        block = wq_block(a, 1 - b, c)
        got(block, agq_r.at[c, 0])
        send(block, block, agq_s.at[c, 3], agq_r.at[c, 1 + 1 - b], right)
        send(block, block, agq_s.at[c, 4], agq_r.at[c, 3 + 1 - b], left)

    def pass_chunk(c):
        block = wq_block(at_x(3), 1, c)
        got(block, agq_r.at[c, 2])
        send(block, block, agq_s.at[c, 5], agq_r.at[c, 5], right)
        block = wq_block(at_x(1), 0, c)
        got(block, agq_r.at[c, 3])
        send(block, block, agq_s.at[c, 6], agq_r.at[c, 6], left)

    def have_chunk(c):
        got(wq_block(at_x(3), 0, c), agq_r.at[c, 1])
        got(wq_block(at_x(1), 1, c), agq_r.at[c, 4])
        got(wq_block(at_x(2), 1, c), agq_r.at[c, 5])
        got(wq_block(at_x(2), 0, c), agq_r.at[c, 6])

    def wo_rows(x_at, z_at, half=None):
        start = (x_at * 2 + z_at) * OROWS
        if half is None:
            return wo.at[pl.ds(pl.multiple_of(start, OROWS), OROWS)]
        return wo.at[pl.ds(pl.multiple_of(start + half * HALF, HALF), HALF)]

    def own_out():
        dst = wo_rows(a, b)
        send(wo_ref, dst, ago_s.at[0], ago_r.at[0], right)
        send(wo_ref, dst, ago_s.at[1], ago_r.at[1], left)
        send(wo_ref, dst, ago_s.at[2], ago_r.at[2], across)

    def pass_out():
        block, part = wo_rows(at_x(3), b), wo_rows(at_x(3), b, 0)
        got(block, ago_r.at[0])
        send(part, part, ago_s.at[3], ago_r.at[3], right)
        send(block, block, ago_s.at[5], ago_r.at[5], across)
        block, part = wo_rows(at_x(1), b), wo_rows(at_x(1), b, 1)
        got(block, ago_r.at[1])
        send(part, part, ago_s.at[4], ago_r.at[4], left)
        send(block, block, ago_s.at[6], ago_r.at[6], across)

    def pass_out_far():
        for half in range(2):
            part = wo_rows(at_x(2), b, half)
            got(part, ago_r.at[3 + half])
            send(part, part, ago_s.at[7 + half], ago_r.at[7 + half], across)

    def have_out():
        got(wo_rows(a, 1 - b), ago_r.at[2])
        got(wo_rows(at_x(3), 1 - b), ago_r.at[5])
        got(wo_rows(at_x(1), 1 - b), ago_r.at[6])
        for half in range(2):
            got(wo_rows(at_x(2), 1 - b, half), ago_r.at[7 + half])

    def island_send():
        @pl.loop(1, islands)
        def _(step):
            to = lax.rem(me + step, islands)
            peer = {"island": to}
            for n, (src, dst) in enumerate((
                (i_send.at[to], i_recv.at[me]),
                (wo_ref.at[:, rows_of(to, oshare)], io_recv.at[me]),
                (g_rows.at[0], ig_recv.at[me]),
            )):
                pltpu.make_async_remote_copy(
                    src_ref=src, dst_ref=dst, send_sem=is_s.at[n, step], recv_sem=is_r.at[n, step],
                    device_id=peer, device_id_type=MESH,
                ).start()
        i_recv[me] = i_send[me]
        io_recv[me] = wo_ref[:, rows_of(me, oshare)]
        ig_recv[me] = g_rows[0]

    def island_sum():
        @pl.loop(1, islands)
        def _(step):
            source = lax.rem(me - step + islands, islands)
            got(i_recv.at[source], is_r.at[0, step])
            got(io_recv.at[source], is_r.at[1, step])
            got(ig_recv.at[source], is_r.at[2, step])
        totq_ref[...] = i_recv[0].astype(F32)
        toto_ref[...] = io_recv[0].astype(F32)
        total = ig_recv[0]
        for i in range(1, islands):
            total = total + ig_recv[i]
        for i in range(8):
            totg_ref[:, i * 256 : (i + 1) * 256] = total[i : i + 1, :]

        @pl.loop(1, islands)
        def _(i):
            totq_ref[...] += i_recv[i].astype(F32)
            toto_ref[...] += io_recv[i].astype(F32)

        i_new[...] = nesterov(qglob_ref[...], qmom_ref[...], totq_ref[...] * (1.0 / islands))[0].astype(BF16)
        io_new[...] = nesterov(oglob_ref[...], omom_ref[...], toto_ref[...] * (1.0 / islands))[0].astype(BF16)

        @pl.loop(1, islands)
        def _(step):
            peer = {"island": lax.rem(me + step, islands)}
            for n, (src, dst) in enumerate(((i_new, i_back.at[me]), (io_new, io_back.at[me]))):
                pltpu.make_async_remote_copy(
                    src_ref=src, dst_ref=dst, send_sem=ib_s.at[n, step], recv_sem=ib_r.at[n, step],
                    device_id=peer, device_id_type=MESH,
                ).start()
        i_back[me] = i_new[...]
        io_back[me] = io_new[...]

    def island_whole():
        @pl.loop(1, islands)
        def _(step):
            source = lax.rem(me - step + islands, islands)
            got(i_back.at[source], ib_r.at[0, step])
            got(io_back.at[source], ib_r.at[1, step])
        for i in range(islands):
            wholeq_ref[:, i * qshare : (i + 1) * qshare] = i_back[i]
            wholeo_ref[:, i * oshare : (i + 1) * oshare] = io_back[i]

        @pl.loop(1, islands)
        def _(step):
            to = lax.rem(me + step, islands)
            left_here(i_send.at[to], is_s.at[0, step])
            left_here(wo_ref.at[:, rows_of(to, oshare)], is_s.at[1, step])
            left_here(g_rows.at[0], is_s.at[2, step])
            left_here(i_new, ib_s.at[0, step])
            left_here(io_new, ib_s.at[1, step])

    def normalise():
        @pl.loop(0, TOK // 128)
        def _(t):
            rows = rows_of(t, 128)
            wide = x_ref[rows, :].astype(F32)
            factor = lax.rsqrt(jnp.mean(wide * wide, axis=-1, keepdims=True) + NORM_EPS)
            fac[rows, :] = factor
            normed = (wide * factor * gain_ref[...]).astype(BF16)
            nrm[rows, :] = normed
            nrm_t[:, rows] = normed.astype(F32).T.astype(BF16)

    def turn(first, second, sign):
        cosine, sine = cos_ref[...], sin_ref[...] * sign
        return first * cosine - second * sine, first * sine + second * cosine

    def project(c):
        mixed = jnp.dot(nrm[...], wq[:, c * COLS : (c + 1) * COLS], preferred_element_type=F32)
        if c == VCHUNK:
            mixed = mixed.astype(BF16).astype(F32)
        mixed_t = mixed.T
        for n in range(COLS // HEAD_DIM):
            at = n * HEAD_DIM
            head = mixed_t[at : at + HEAD_DIM, :]
            if c != VCHUNK:
                first, second = turn(head[: HEAD_DIM // 2], head[HEAD_DIM // 2 :], 1.0)
                head = jnp.concatenate([first, second], axis=0)
            held = head.astype(BF16)
            if c < KCHUNK:
                held = (held.astype(F32) * HEAD_DIM ** (-0.5)).astype(BF16)
            qkv_t[c * COLS + at : c * COLS + at + HEAD_DIM, :] = held
            if c == KCHUNK:
                k_tok[n] = held.astype(F32).T.astype(BF16)
            if c == VCHUNK:
                v_tok[n] = held.astype(F32).T.astype(BF16)

    def project_back():
        @pl.loop(0, 8)
        def _(j):
            rows = rows_of(j, OROWS)
            datt_t[rows, :] = lax.dot_general(
                wo[rows, :], cot_ref[...], NT, preferred_element_type=F32
            ).astype(BF16)

    def attend(g):
        krows = slice(QW + g * HEAD_DIM, QW + (g + 1) * HEAD_DIM)
        vrows = slice(QW + (KV_HEADS + g) * HEAD_DIM, QW + (KV_HEADS + g + 1) * HEAD_DIM)
        dk_acc[...] = jnp.zeros_like(dk_acc)
        dv_acc[...] = jnp.zeros_like(dv_acc)

        @pl.loop(0, GROUP)
        def _(n):
            rows = rows_of(g * GROUP + n, HEAD_DIM)
            for q_at in range(0, TOK, QB):
                keys = q_at + QB
                queries = qkv_t[rows, q_at : q_at + QB]
                scores = jnp.dot(k_tok[g, :keys, :], queries, preferred_element_type=F32)
                key_at = lax.broadcasted_iota(jnp.int32, (keys, QB), 0)
                query_at = lax.broadcasted_iota(jnp.int32, (keys, QB), 1) + q_at
                scores = jnp.where(query_at >= key_at, scores, -1e30)
                top = jnp.max(scores, axis=0, keepdims=True)
                raised = jnp.exp(scores - top)
                soft = raised * (1.0 / jnp.sum(raised, axis=0, keepdims=True))
                weights = soft.astype(BF16)
                out = jnp.dot(qkv_t[vrows, :keys], weights, preferred_element_type=F32)
                att_t[rows, q_at : q_at + QB] = out.astype(BF16)
                dout = datt_t[rows, q_at : q_at + QB]
                dweights = jnp.dot(v_tok[g, :keys, :], dout, preferred_element_type=F32)
                dot_out = jnp.sum(out * dout.astype(F32), axis=0, keepdims=True)
                dscores = (soft * (dweights - dot_out)).astype(BF16)
                dqueries = jnp.dot(qkv_t[krows, :keys], dscores, preferred_element_type=F32)
                dqueries = (dqueries * HEAD_DIM ** (-0.5)).astype(BF16).astype(F32)
                half = HEAD_DIM // 2
                cosine, sine = cos_ref[:, q_at : q_at + QB], sin_ref[:, q_at : q_at + QB]
                first, second = dqueries[:half], dqueries[half:]
                dm_t[rows, q_at : q_at + QB] = jnp.concatenate(
                    [first * cosine + second * sine, second * cosine - first * sine], axis=0
                ).astype(BF16)
                dk_acc[:, :keys] += lax.dot_general(queries, dscores, NT, preferred_element_type=F32)
                dv_acc[:, :keys] += lax.dot_general(dout, weights, NT, preferred_element_type=F32)

        dkeys = dk_acc[...].astype(BF16).astype(F32)
        first, second = turn(dkeys[: HEAD_DIM // 2], dkeys[HEAD_DIM // 2 :], -1.0)
        dm_t[krows, :] = jnp.concatenate([first, second], axis=0).astype(BF16)
        dm_t[vrows, :] = dv_acc[...].astype(BF16)

    def gq_block(x_at, z_at, c):
        return gq.at[rows_of(x_at * 2 + z_at, QROWS), pl.ds(c * COLS, COLS)]

    def rq_at(n, c):
        return rq.at[n, :, pl.ds(c * COLS, COLS)]

    def grad_chunk(c):
        cols = slice(c * COLS, (c + 1) * COLS)

        @pl.loop(0, 8)
        def _(j):
            rows = rows_of(j, QROWS)
            gq[rows, cols] = lax.dot_general(
                nrm_t[rows, :], dm_t[cols, :], NT, preferred_element_type=F32
            ).astype(BF16)

        for n, (block, to) in enumerate((
            (gq_block(at_x(2), 0, c), left),
            (gq_block(at_x(2), 1, c), right),
            (gq_block(at_x(3), 1, c), left),
            (gq_block(at_x(1), 0, c), right),
        )):
            send(block, rq_at(n, c), rsq_s.at[c, n], rsq_r.at[c, n], to)
        dm[:, cols] = dm_t[cols, :].astype(F32).T.astype(BF16)

    def add_chunk(c):
        for n, (block, to) in enumerate(((gq_block(at_x(3), 0, c), left), (gq_block(at_x(1), 1, c), right))):
            got(rq_at(n, c), rsq_r.at[c, n])
            block[...] = (block[...].astype(F32) + rq_at(n, c)[...].astype(F32)).astype(BF16)
            send(block, rq_at(4 + n, c), rsq_s.at[c, 4 + n], rsq_r.at[c, 4 + n], to)

    def fold_chunk(c):
        for n in range(2, 6):
            got(rq_at(n, c), rsq_r.at[c, n])

        def whole(z_at, first, second):
            return (
                gq_block(a, z_at, c)[...].astype(F32)
                + rq.at[first, :, pl.ds(c * COLS, COLS)][...].astype(F32)
                + rq.at[second, :, pl.ds(c * COLS, COLS)][...].astype(F32)
            )

        block = gq_block(a, 1 - b, c)
        block[...] = whole(1 - b, 2 + b, 5 - b).astype(BF16)
        send(block, rq_at(6, c), rsq_s.at[c, 6], rsq_r.at[c, 6], across)
        sumq_ref[:, c * COLS : (c + 1) * COLS] = whole(b, 3 - b, 4 + b)

    def end_chunk(c):
        got(rq_at(6, c), rsq_r.at[c, 6])
        sumq_ref[:, c * COLS : (c + 1) * COLS] += rq_at(6, c)[...].astype(F32)

    def go_rows(x_at, z_at, half=None):
        start = (x_at * 2 + z_at) * OROWS
        if half is None:
            return go.at[pl.ds(pl.multiple_of(start, OROWS), OROWS)]
        return go.at[pl.ds(pl.multiple_of(start + half * HALF, HALF), HALF)]

    def grad_out(g):
        @pl.loop(0, 2)
        def _(z_at):
            rows = rows_of(2 * g + z_at, OROWS)
            go[rows, :] = jnp.dot(att_t[rows, :], cot_ref[...], preferred_element_type=F32).astype(BF16)

        send(go_rows(g, 1 - b), ro_z.at[g], rso_s.at[6 + g], rso_r.at[6 + g], across)

    def pair_out(step):
        x_at = at_x(step)
        got(ro_z.at[x_at], rso_r.at[6 + x_at])
        block = go_rows(x_at, b)
        block[...] = (block[...].astype(F32) + ro_z[x_at].astype(F32)).astype(BF16)

    def ring_out():
        pair_out(2)
        send(go_rows(at_x(2), b, 0), ro.at[0], rso_s.at[0], rso_r.at[0], left)
        send(go_rows(at_x(2), b, 1), ro.at[1], rso_s.at[1], rso_r.at[1], right)
        pair_out(3)
        send(go_rows(at_x(3), b, 1), ro.at[2], rso_s.at[2], rso_r.at[2], left)
        pair_out(1)
        send(go_rows(at_x(1), b, 0), ro.at[3], rso_s.at[3], rso_r.at[3], right)
        pair_out(0)

    def add_out():
        for n, (block, to) in enumerate(((go_rows(at_x(3), b, 0), left), (go_rows(at_x(1), b, 1), right))):
            got(ro.at[n], rso_r.at[n])
            block[...] = (block[...].astype(F32) + ro[n].astype(F32)).astype(BF16)
            send(block, ro.at[4 + n], rso_s.at[4 + n], rso_r.at[4 + n], to)

    def end_out():
        for n in range(2, 6):
            got(ro.at[n], rso_r.at[n])
        sumo_ref[:HALF, :] = go_rows(a, b, 0)[...].astype(F32) + ro[3].astype(F32) + ro[4].astype(F32)
        sumo_ref[HALF:, :] = go_rows(a, b, 1)[...].astype(F32) + ro[2].astype(F32) + ro[5].astype(F32)

    def gain_grad():
        @pl.loop(0, 8)
        def _(j):
            dnormed = lax.dot_general(
                dm[...], wq[rows_of(j, QROWS), :], NT, preferred_element_type=F32
            ).astype(BF16).astype(F32)
            wide = x_ref[:, rows_of(j, QROWS)].astype(F32) * fac[...]
            g_rows[1, pl.ds(j, 1), :] = jnp.sum(dnormed * wide, axis=0, keepdims=True)

        @pl.loop(1, 8)
        def _(step):
            pltpu.make_async_remote_copy(
                src_ref=g_rows.at[1], dst_ref=g_recv.at[f], send_sem=gg_s.at[step], recv_sem=gg_r.at[step],
                device_id={"fsdp": lax.rem(f + step, 8)}, device_id_type=MESH,
            ).start()
        g_recv[f] = g_rows[1]

    def gain_sum():
        @pl.loop(1, 8)
        def _(step):
            got(g_recv.at[lax.rem(f - step + 8, 8)], gg_r.at[step])
        total = g_recv[0]
        for i in range(1, 8):
            total = total + g_recv[i]
        for i in range(8):
            sumg_ref[:, i * 256 : (i + 1) * 256] = total[i : i + 1, :]

        @pl.loop(1, 8)
        def _(step):
            left_here(g_rows.at[1], gg_s.at[step])

    for i in range(8):
        g_rows[0, i : i + 1, :] = gain_ref[:, i * 256 : (i + 1) * 256]
    keep = [
        pltpu.make_async_copy(wq_ref, wq.at[rows_of(f, QROWS)], own_sem.at[0]),
        pltpu.make_async_copy(wo_ref, wo.at[rows_of(f, OROWS)], own_sem.at[1]),
    ]
    order = [KCHUNK, VCHUNK, 0, 1, 2, 3]
    own_chunk(order[0])
    own_out()
    own_chunk(order[1])
    for copy in keep:
        copy.start()
    island_send()
    normalise()
    for copy in keep:
        copy.wait()
    pair_chunk(order[0])
    pass_out()
    own_chunk(order[2])
    pair_chunk(order[1])
    pass_chunk(order[0])
    pass_out_far()
    own_chunk(order[3])
    pair_chunk(order[2])
    pass_chunk(order[1])
    have_chunk(order[0])
    project(order[0])
    own_chunk(order[4])
    pair_chunk(order[3])
    pass_chunk(order[2])
    have_chunk(order[1])
    project(order[1])
    island_sum()
    own_chunk(order[5])
    pair_chunk(order[4])
    pass_chunk(order[3])
    have_out()
    project_back()
    have_chunk(order[2])
    project(order[2])
    pair_chunk(order[5])
    pass_chunk(order[4])
    attend(0)
    grad_chunk(0)
    grad_out(0)
    pass_chunk(order[5])
    have_chunk(order[3])
    project(order[3])
    add_chunk(0)
    attend(1)
    grad_chunk(1)
    grad_out(1)
    have_chunk(order[4])
    project(order[4])
    add_chunk(1)
    fold_chunk(0)
    attend(2)
    grad_chunk(2)
    grad_out(2)
    have_chunk(order[5])
    project(order[5])
    add_chunk(2)
    fold_chunk(1)
    attend(3)
    grad_out(3)
    grad_chunk(3)
    grad_chunk(KCHUNK)
    grad_chunk(VCHUNK)
    add_chunk(3)
    fold_chunk(2)
    ring_out()
    add_chunk(KCHUNK)
    fold_chunk(3)
    add_chunk(VCHUNK)
    add_out()
    gain_grad()
    end_chunk(0)
    end_chunk(1)
    fold_chunk(KCHUNK)
    island_whole()
    fold_chunk(VCHUNK)
    end_chunk(2)
    end_chunk(3)
    end_out()
    end_chunk(KCHUNK)
    gain_sum()
    end_chunk(VCHUNK)
    for src, s_sem in sent:
        left_here(src, s_sem)


def grads(islands, x, cot, gain, wq, wo, qglob, qmom, oglob, omom):
    qshare, oshare = QKV // islands, D // islands
    cosine, sine = rope_tables()
    vmem = pl.BlockSpec(memory_space=pltpu.VMEM)
    dma = pltpu.SemaphoreType.DMA
    return pl.pallas_call(
        functools.partial(grads_kernel, islands),
        out_shape=[
            jax.ShapeDtypeStruct((QROWS, QKV), F32),
            jax.ShapeDtypeStruct((OROWS, D), F32),
            jax.ShapeDtypeStruct((1, D), F32),
            jax.ShapeDtypeStruct((QROWS, qshare), F32),
            jax.ShapeDtypeStruct((OROWS, oshare), F32),
            jax.ShapeDtypeStruct((1, D), F32),
            jax.ShapeDtypeStruct((QROWS, QKV), BF16),
            jax.ShapeDtypeStruct((OROWS, D), BF16),
        ],
        in_specs=[vmem] * 11,
        out_specs=[vmem] * 8,
        scratch_shapes=[
            pltpu.VMEM((D, QKV), BF16),
            pltpu.VMEM((QW, D), BF16),
            pltpu.VMEM((TOK, D), BF16),
            pltpu.VMEM((D, TOK), BF16),
            pltpu.VMEM((TOK, 1), F32),
            pltpu.VMEM((QKV, TOK), BF16),
            pltpu.VMEM((KV_HEADS, TOK, HEAD_DIM), BF16),
            pltpu.VMEM((KV_HEADS, TOK, HEAD_DIM), BF16),
            pltpu.VMEM((QW, TOK), BF16),
            pltpu.VMEM((QW, TOK), BF16),
            pltpu.VMEM((QKV, TOK), BF16),
            pltpu.VMEM((TOK, QKV), BF16),
            pltpu.VMEM((HEAD_DIM, TOK), F32),
            pltpu.VMEM((HEAD_DIM, TOK), F32),
            pltpu.VMEM((D, QKV), BF16),
            pltpu.VMEM((QW, D), BF16),
            pltpu.VMEM((7, QROWS, QKV), BF16),
            pltpu.VMEM((6, HALF, D), BF16),
            pltpu.VMEM((4, OROWS, D), BF16),
            pltpu.VMEM((2, 8, 256), F32),
            pltpu.VMEM((8, 8, 256), F32),
            pltpu.VMEM((islands, QROWS, qshare), BF16),
            pltpu.VMEM((islands, QROWS, qshare), BF16),
            pltpu.VMEM((islands, OROWS, oshare), BF16),
            pltpu.VMEM((islands, 8, 256), F32),
            pltpu.VMEM((islands, QROWS, qshare), BF16),
            pltpu.VMEM((islands, OROWS, oshare), BF16),
            pltpu.VMEM((QROWS, qshare), BF16),
            pltpu.VMEM((OROWS, oshare), BF16),
            dma((2,)),
            dma((CHUNKS, 7)), dma((CHUNKS, 7)),
            dma((9,)), dma((9,)),
            dma((CHUNKS, 7)), dma((CHUNKS, 7)),
            dma((10,)), dma((10,)),
            dma((8,)), dma((8,)),
            dma((3, islands)), dma((3, islands)),
            dma((2, islands)), dma((2, islands)),
        ],
        compiler_params=pltpu.CompilerParams(
            collective_id=0, has_side_effects=True, vmem_limit_bytes=63 * 2**20
        ),
        name="grads",
    )(x, cot, gain, wq, wo, jnp.asarray(cosine), jnp.asarray(sine), qglob, qmom, oglob, omom)


def update_kernel(
    islands,
    gain_ref, wq_ref, wo_ref, gf_ref, gs_ref, qf_ref, qs_ref, of_ref, os_ref,
    gg_ref, gm_ref, qg_ref, qm_ref, og_ref, om_ref,
    sumq_ref, sumo_ref, sumg_ref, totq_ref, toto_ref, totg_ref, wholeq_ref, wholeo_ref,
    gain_o, wq_o, wo_o, gf_o, gs_o, qf_o, qs_o, of_o, os_o, gg_o, gm_o, qg_o, qm_o, og_o, om_o,
):
    scale = 1.0 / islands
    for w, s, m1, m2, whole, w_o, m1_o, m2_o in (
        (wq_ref, sumq_ref, qf_ref, qs_ref, wholeq_ref, wq_o, qf_o, qs_o),
        (wo_ref, sumo_ref, of_ref, os_ref, wholeo_ref, wo_o, of_o, os_o),
    ):
        stepped, first, second = adamw(w[...], s[...], m1[...], m2[...], WEIGHT_DECAY)
        w_o[...] = (MIXING * stepped + (1.0 - MIXING) * whole[...].astype(F32)).astype(BF16)
        m1_o[...] = first
        m2_o[...] = second

    @pl.when(pl.program_id(0) == 0)
    def _():
        stepped, first, second = adamw(gain_ref[...], sumg_ref[...], gf_ref[...], gs_ref[...], 0.0)
        outer, momentum = nesterov(gg_ref[...], gm_ref[...], totg_ref[...] * scale)
        gain_o[...] = MIXING * stepped + (1.0 - MIXING) * outer
        gf_o[...] = first
        gs_o[...] = second
        gg_o[...] = outer
        gm_o[...] = momentum
        qg_o[...], qm_o[...] = nesterov(qg_ref[...], qm_ref[...], totq_ref[...] * scale)
        og_o[...], om_o[...] = nesterov(og_ref[...], om_ref[...], toto_ref[...] * scale)


def update(islands, state, sums):
    steps = 4

    def spec(array):
        rows, cols = array.shape
        if cols in (QKV, D) and rows > 1:
            return pl.BlockSpec((rows // steps, cols), lambda i: (i, 0))
        return pl.BlockSpec((rows, cols), lambda i: (0, 0))

    outs = [state[n] for n in (0, 1, 2, 3, 4, 5, 6, 7, 8, 9, 10, 11, 12, 13, 14)]
    return pl.pallas_call(
        functools.partial(update_kernel, islands),
        grid=(steps,),
        out_shape=[jax.ShapeDtypeStruct(o.shape, o.dtype) for o in outs],
        in_specs=[spec(v) for v in (*state, *sums)],
        out_specs=[spec(o) for o in outs],
        compiler_params=pltpu.CompilerParams(vmem_limit_bytes=32 * 2**20),
        name="update",
    )(*state, *sums)


def shards(
    tokens, cotangent, norm_gain, qkv_weight, out_weight, gain_first, gain_second,
    qkv_first, qkv_second, out_first, out_second,
    gain_global, gain_momentum, qkv_global, qkv_momentum, out_global, out_momentum,
):
    islands = lax.axis_size("island")
    wq, wo = qkv_weight[0], out_weight[0]
    sums = grads(
        islands, tokens, cotangent, norm_gain, wq, wo, qkv_global, qkv_momentum, out_global, out_momentum
    )
    state = (
        norm_gain, wq, wo, gain_first, gain_second, qkv_first[0], qkv_second[0], out_first[0], out_second[0],
        gain_global[None], gain_momentum[None], qkv_global, qkv_momentum, out_global, out_momentum,
    )
    (
        gain_next, wq_next, wo_next, gf, gs, qf, qs, of, os_, gg, gm, qg, qm, og, om
    ) = update(islands, state, sums)
    return (
        gain_next, wq_next[None], wo_next[None], gf, gs, qf[None], qs[None], of[None], os_[None],
        gg[0], gm[0], qg, qm, og, om,
    )


def solution(mesh):
    placed = (
        P(("island", "fsdp"), None),
        P(("island", "fsdp"), None),
        P("island", None),
        P("island", "fsdp", None),
        P("island", "fsdp", None),
        P("island", None),
        P("island", None),
        P("island", "fsdp", None),
        P("island", "fsdp", None),
        P("island", "fsdp", None),
        P("island", "fsdp", None),
        P(),
        P(),
        P("fsdp", "island"),
        P("fsdp", "island"),
        P("fsdp", "island"),
        P("fsdp", "island"),
    )
    return jax.shard_map(
        shards,
        mesh=mesh,
        in_specs=placed,
        out_specs=(
            P("island", None),
            P("island", "fsdp", None),
            P("island", "fsdp", None),
            P("island", None),
            P("island", None),
            P("island", "fsdp", None),
            P("island", "fsdp", None),
            P("island", "fsdp", None),
            P("island", "fsdp", None),
            P(),
            P(),
            P("fsdp", "island"),
            P("fsdp", "island"),
            P("fsdp", "island"),
            P("fsdp", "island"),
        ),
        check_vma=False,
    )
```

time: 555 us -> 235 us (0.42)
  waiting for transfers between devices: 277 us -> 0 us
  Pallas kernels: 0 us -> 209 us
  blocking collectives: 125 us -> 0 us
  matrix products: 68.9 us -> 0 us
  other arithmetic: 43.1 us -> 0 us
  between operations: 16.2 us -> 0.72 us
    all_gather x2 -> x0, waiting for transfers between devices: 214 us -> none  [the longest x1 128 us: inner_step(): lax.all_gather(local_qkv, 'fsdp', axis=0, tiled=True)]
    pallas_call x0 -> x2, Pallas kernels: none -> 209 us  [the longest x1 205 us: grads(): pl.pallas_call(functools.partial(grads_kernel, islands), out_shape=[jax.S...]
    all_gather x2 -> x0, blocking collectives: 72.1 us -> none  [the longest x1 39.3 us: outer_sync(): lax.all_gather(qkv_pair[0].astype(jnp.bfloat16), 'island', axis=1, tiled=...]
    dot_general x11 -> x0, matrix products: 68.9 us -> none  [the longest x3 24.2 us: attend_part(): jnp.einsum('kgqs,skd->qkgd', weights, values, preferred_element_type=jnp....]
    reduce_scatter x2 -> x0, waiting for transfers between devices: 60.7 us -> none  [the longest x1 60.7 us: inner_step(): lax.psum_scatter(g_qkv.astype(jnp.float32).astype(jnp.bfloat16), 'fsdp',...]
    psum x2 -> x0, blocking collectives: 53.3 us -> none  [the longest x1 34.7 us: outer_sync(): gain_total = lax.psum(gain, 'island')]
    unnamed x72 -> x50, local copies, waits for them, and re-layouts: 9.88 us -> 24.2 us
    reduce_sum x2 -> x0, other arithmetic: 11.8 us -> none  [the longest x1 9.77 us: attend_part(): weights = jax.nn.softmax(scores, axis=-1).astype(jnp.bfloat16)]
  transfers between devices with their start and end apart: 6 -> 0, of which waited for: 3 -> 0; matrix products, arithmetic and copies ran while one was open for 23% -> 0% of each run, Pallas kernels for 0% -> 0%
where the time goes in v1:
time: 235 us; the launch traced here: 234 us
  Pallas kernels  209 us (89%)
  local copies, waits for them, and re-layouts  24.2 us (10%)
    pallas_call x1, Pallas kernels, grads(): pl.pallas_call(functools.partial(grads_kernel, islands), out_shape=[jax.S...  205 us
    unnamed x50, local copies, waits for them, and re-layouts  24.2 us

profile of v1, /device:TPU:64, one launch (start us, length us, event | category | flops | bytes accessed | tf_op | source)
XLA Modules:
  0.0 234.3 jit_solution(14895750325857767852)
XLA Ops:
  0.6 1.6 copy.36.qglob_ref.qg_ref
  2.3 1.6 copy.37.qmom_ref.qm_ref
  3.9 0.0 copy-start
  3.9 0.0 copy-start.5
  3.9 205.1 %grads.1 = (f32[256,1536]{1,0:T(8,128)}, f32[128,2048]{1,0:T(8,128)}, f32[1,2048]{1,0:T(1,128)}, f32[256,96]{1,0:T(8,128)}, f32[128,128]{1,0:T(8,128)}, /*index=...) custom-call(bf16[512,2048]{1,0:T(8,128)(2,1)} %x_ref.1, bf16[512,2048]{1,0:T(8,128)(2,1)} %cot_ref.1, ...), custom_call_target="tpu_custom_call" | custom-call | tf_op jit(solution)/shard_map/grads/pallas_call | solution.py:572
  209.0 0.0 copy-done
  209.0 0.0 copy-done.5
  209.0 0.0 copy-done.12
  209.0 0.0 copy-start.1
  209.1 1.0 copy-done.1
  210.1 1.4 copy-done.2
  211.5 1.4 copy-done.3
  212.9 1.4 copy-done.4
  214.3 0.9 copy-done.6
  215.2 1.2 copy-done.7
  216.4 1.2 copy-done.8
  217.7 1.2 copy-done.9
  218.9 1.1 copy-done.10
  220.0 1.0 copy-done.11
  221.1 0.8 copy-done.13
  221.9 0.9 copy-done.14
  222.8 0.8 copy-done.15
  223.7 0.7 copy-done.16
  224.4 0.7 copy-done.17
  225.1 0.7 copy-done.18
  225.7 0.7 copy-done.19
  226.4 0.7 copy-done.20
  227.1 0.7 copy-done.21
  227.8 0.7 copy-done.22
  228.5 4.3 %update.1 = (f32[1,2048]{1,0:T(1,128)}, bf16[256,1536]{1,0:T(8,128)(2,1)}, bf16[128,2048]{1,0:T(8,128)(2,1)}, f32[1,2048]{1,0:T(1,128)}, f32[1,2048]{1,0:T(1,128...) custom-call(f32[1,2048]{1,0:T(1,128)S(1)} %copy-done.16, ...), custom_call_target="tpu_custom_call" | custom-call | tf_op jit(solution)/shard_map/update/pallas_call | solution.py:672
  232.9 0.7 copy.38
  233.6 0.7 copy.39
  (20 shorter events, 0.0 us)
Async XLA Ops:
  3.9 205.1 %copy-start = (bf16[1,256,1536]{2,1,0:T(8,128)(2,1)S(1)}, bf16[1,256,1536]{2,1,0:T(8,128)(2,1)}, u32[]{:S(2)}) copy-start(bf16[1,256,1536]{2,1,0:T(8,128)(2,1)} %param.22) | copy-start | bytes 2359300
  3.9 205.1 %copy-start.5 = (f32[256,96]{1,0:T(8,128)S(1)}, f32[256,96]{1,0:T(8,128)}, u32[]{:S(2)}) copy-start(f32[256,96]{1,0:T(8,128)} %copy.36.qglob_ref.qg_ref) | copy-start | bytes 294916
  3.9 205.1 %copy-start.12 = (f32[128,128]{1,0:T(8,128)S(1)}, f32[128,128]{1,0:T(8,128)}, u32[]{:S(2)}) copy-start(f32[128,128]{1,0:T(8,128)} %og_ref.1) | copy-start | bytes 196612
  209.0 1.0 copy-start.1
  210.1 1.4 copy-start.2
  211.5 1.4 copy-start.3
  212.9 1.4 copy-start.4
  214.3 0.9 copy-start.6
  215.2 1.2 copy-start.7
  216.4 1.2 copy-start.8
  217.7 1.2 copy-start.9
  218.9 1.1 copy-start.10
  220.0 1.0 copy-start.11
  221.1 0.8 copy-start.13
  221.9 0.9 copy-start.14
  222.8 0.8 copy-start.15
  223.7 0.7 copy-start.16
  224.4 0.7 copy-start.17
  225.0 0.7 copy-start.18
  225.7 0.7 copy-start.19
  226.4 0.7 copy-start.20
  227.1 0.7 copy-start.21
  227.8 0.7 copy-start.22

commit v2 on v1

v2 whole, which is shorter than its diff:
```python
import functools

import jax
import jax.numpy as jnp
import numpy as np
from jax import lax
from jax.experimental import pallas as pl
from jax.experimental.pallas import tpu as pltpu
from jax.sharding import PartitionSpec as P

HEADS = 16
KV_HEADS = 4
HEAD_DIM = 64
GROUP = HEADS // KV_HEADS

BETA_ONE = 0.9
BETA_TWO = 0.95
ADAM_EPS = 1e-08
INNER_RATE = 0.001
WEIGHT_DECAY = 0.1
STEP_COUNT = 100.0
OUTER_RATE = 0.7
OUTER_MOMENTUM = 0.9
MIXING = 0.5
NORM_EPS = 1e-05
ROPE_BASE = 500000.0

MESH = pl.DeviceIdType.MESH
F32 = jnp.float32
BF16 = jnp.bfloat16

TOK = 512
D = 2048
QW = HEADS * HEAD_DIM
QKV = QW + 2 * KV_HEADS * HEAD_DIM
QROWS = 256
OROWS = 128
HALF = OROWS // 2
OPAIRED = 512
COLS = 256
CHUNKS = QKV // COLS
KCHUNK, VCHUNK = QW // COLS, QW // COLS + 1
QB = 256
NT = (((1,), (1,)), ((), ()))


def rope_tables():
    half = HEAD_DIM // 2
    freqs = ROPE_BASE ** (-np.arange(half, dtype=np.float64) / half)
    angles = freqs[:, None] * np.arange(TOK, dtype=np.float64)[None, :]
    return np.cos(angles).astype(np.float32), np.sin(angles).astype(np.float32)


def adamw(param, grad, first, second, decay):
    wide = param.astype(F32)
    first_next = BETA_ONE * first + (1.0 - BETA_ONE) * grad
    second_next = BETA_TWO * second + (1.0 - BETA_TWO) * grad * grad
    update = (
        first_next
        * (1.0 / (1.0 - BETA_ONE**STEP_COUNT))
        / (jnp.sqrt(second_next * (1.0 / (1.0 - BETA_TWO**STEP_COUNT))) + ADAM_EPS)
    )
    return (wide - INNER_RATE * (update + decay * wide), first_next, second_next)


def nesterov(global_value, momentum, average):
    delta = global_value - average
    momentum_next = OUTER_MOMENTUM * momentum + delta
    return (global_value - OUTER_RATE * (delta + OUTER_MOMENTUM * momentum_next), momentum_next)


def rows_of(index, size):
    return pl.ds(pl.multiple_of(index * size, size), size)


def grads_kernel(
    islands,
    x_in, cot_in, gain_in, wq_in, wo_in, cos_in, sin_in, qglob_in, qmom_in, oglob_in, omom_in,
    sumq_out, sumo_out, sumg_out, totq_out, toto_out, totg_out, wholeq_out, wholeo_out,
    x_ref, cot_ref, gain_ref, cos_ref, sin_ref, qglob_ref, qmom_ref, oglob_ref, omom_ref,
    sumq_ref, sumo_ref, sumg_ref, totq_ref, toto_ref, totg_ref, wholeq_ref, wholeo_ref,
    wq, wo, nrm, nrm_t, fac, qkv_t, k_tok, v_tok, datt_t, att_t, dm_t, dm, dk_acc, dv_acc,
    gq, go, rq, ro, ro_z, g_rows, g_recv,
    i_own, io_own, i_core, io_core, ig_core, i_ring, io_ring, ig_ring, i_far, io_far, ig_far, ig_own, i_back, io_back,
    own_sem, out_sem, agq_s, agq_r, ago_s, ago_r, rsq_s, rsq_r, rso_s, rso_r, gg_s, gg_r, is_s, is_r,
):
    f = lax.axis_index("fsdp")
    me = lax.axis_index("island")
    a, b = f // 2, f % 2
    y, zh, core = me // 4, (me // 2) % 2, me % 2
    qshare = QKV // islands
    oshare = D // islands

    def at_x(step):
        return lax.rem(a + step, 4)

    right = {"fsdp": at_x(1) * 2 + b}
    left = {"fsdp": at_x(3) * 2 + b}
    across = {"fsdp": a * 2 + 1 - b}
    sent = []

    def send(src, dst, s_sem, r_sem, to):
        copy = pltpu.make_async_remote_copy(
            src_ref=src, dst_ref=dst, send_sem=s_sem, recv_sem=r_sem, device_id=to, device_id_type=MESH
        )
        copy.start()
        sent.append((src, s_sem))

    def got(dst, r_sem):
        pltpu.make_async_remote_copy(
            src_ref=dst, dst_ref=dst, send_sem=r_sem, recv_sem=r_sem, device_id=across, device_id_type=MESH
        ).wait_recv()

    def left_here(src, s_sem):
        pltpu.make_async_remote_copy(
            src_ref=src, dst_ref=src, send_sem=s_sem, recv_sem=s_sem, device_id=across, device_id_type=MESH
        ).wait_send()

    barrier = pltpu.get_barrier_semaphore()

    @pl.loop(1, 8)
    def _(step):
        pl.semaphore_signal(barrier, inc=1, device_id={"fsdp": lax.rem(f + step, 8)}, device_id_type=MESH)

    other_core = {"island": me + 1 - 2 * core}
    other_far = {"island": me + 2 - 4 * zh}

    def other_y(step):
        return lax.rem(y + step, 4)

    def on_y(step):
        return {"island": other_y(step) * 4 + zh * 2 + core}

    pl.semaphore_signal(barrier, inc=1, device_id=other_core, device_id_type=MESH)
    pl.semaphore_signal(barrier, inc=1, device_id=other_far, device_id_type=MESH)
    for step in range(1, 4):
        pl.semaphore_signal(barrier, inc=1, device_id=on_y(step), device_id_type=MESH)
    loads = [
        pltpu.make_async_copy(src, dst, own_sem.at[n])
        for n, (src, dst) in enumerate((
            (x_in, x_ref), (gain_in, gain_ref), (wq_in, wq.at[rows_of(f, QROWS)]), (wo_in, wo.at[rows_of(f, OROWS)]),
            (cos_in, cos_ref), (sin_in, sin_ref), (cot_in, cot_ref), (qglob_in, qglob_ref), (qmom_in, qmom_ref),
            (oglob_in, oglob_ref), (omom_in, omom_ref),
        ))
    ]
    for copy in loads:
        copy.start()
    stores = []

    def store(src, dst):
        copy = pltpu.make_async_copy(src, dst, out_sem.at[len(stores)])
        copy.start()
        stores.append(copy)

    pl.semaphore_wait(barrier, 7 + 5)

    def wq_block(c):
        def block(x_at, z_at, half=None):
            start, size = (x_at * 2 + z_at) * QROWS, QROWS
            if half is not None:
                start, size = start + half * (QROWS // 2), QROWS // 2
            return wq.at[pl.ds(pl.multiple_of(start, size), size), pl.ds(c * COLS, COLS)]

        return block

    def wo_block(col, cols):
        def block(x_at, z_at, half=None):
            start, size = (x_at * 2 + z_at) * OROWS, OROWS
            if half is not None:
                start, size = start + half * HALF, HALF
            return wo.at[pl.ds(pl.multiple_of(start, size), size), pl.ds(col, cols)]

        return block

    class Paired:
        def __init__(self, src, block, n):
            self.src, self.block, self.s, self.r = src, block, agq_s.at[n], agq_r.at[n]

        def own(self):
            dst = self.block(a, b)
            send(self.src, dst, self.s.at[0], self.r.at[0], across)
            send(self.src, dst, self.s.at[1], self.r.at[1 + b], right)
            send(self.src, dst, self.s.at[2], self.r.at[3 + b], left)

        def pair(self):
            block = self.block(a, 1 - b)
            got(block, self.r.at[0])
            send(block, block, self.s.at[3], self.r.at[1 + 1 - b], right)
            send(block, block, self.s.at[4], self.r.at[3 + 1 - b], left)

        def onward(self):
            block = self.block(at_x(3), 1)
            got(block, self.r.at[2])
            send(block, block, self.s.at[5], self.r.at[5], right)
            block = self.block(at_x(1), 0)
            got(block, self.r.at[3])
            send(block, block, self.s.at[6], self.r.at[6], left)

        def have(self):
            got(self.block(at_x(3), 0), self.r.at[1])
            got(self.block(at_x(1), 1), self.r.at[4])
            got(self.block(at_x(2), 1), self.r.at[5])
            got(self.block(at_x(2), 0), self.r.at[6])

    class Ringed:
        def __init__(self, src, block, n):
            self.src, self.block, self.s, self.r = src, block, ago_s.at[n], ago_r.at[n]

        def own(self):
            dst = self.block(a, b)
            send(self.src, dst, self.s.at[0], self.r.at[0], right)
            send(self.src, dst, self.s.at[1], self.r.at[1], left)
            send(self.src, dst, self.s.at[2], self.r.at[2], across)

        def onward(self):
            for n, (x_at, to) in enumerate(((at_x(3), right), (at_x(1), left))):
                block, part = self.block(x_at, b), self.block(x_at, b, n)
                got(block, self.r.at[n])
                send(part, part, self.s.at[3 + n], self.r.at[3 + n], to)
                send(block, block, self.s.at[5 + n], self.r.at[5 + n], across)

        def far(self):
            for n in range(2):
                part = self.block(at_x(2), b, n)
                got(part, self.r.at[3 + n])
                send(part, part, self.s.at[7 + n], self.r.at[7 + n], across)

        def have(self):
            got(self.block(a, 1 - b), self.r.at[2])
            got(self.block(at_x(3), 1 - b), self.r.at[5])
            got(self.block(at_x(1), 1 - b), self.r.at[6])
            for n in range(2):
                got(self.block(at_x(2), 1 - b, n), self.r.at[7 + n])

    chunks = [
        (Paired if c != 3 else Ringed)(wq_in.at[:, pl.ds(c * COLS, COLS)], wq_block(c), c if c != 3 else 1)
        for c in range(CHUNKS)
    ]
    out_paired = Paired(wo_in.at[:, pl.ds(0, OPAIRED)], wo_block(0, OPAIRED), 3)
    out_ringed = Ringed(wo_in.at[:, pl.ds(OPAIRED, D - OPAIRED)], wo_block(OPAIRED, D - OPAIRED), 0)

    def island_start():
        own = wq.at[rows_of(f, QROWS)]
        for i in range(islands):
            if i % 4 == 0:
                turned = own[:, i * qshare : (i + 4) * qshare].astype(F32).T.astype(BF16)
            i_own[i // 2, i % 2] = turned[i % 4 * qshare : (i % 4 + 1) * qshare]
            io_own[i // 2, i % 2] = wo[rows_of(f, OROWS), i * oshare : (i + 1) * oshare]
        for i in range(8):
            ig_own[i : i + 1, :] = gain_ref[:, i * 256 : (i + 1) * 256]
        send(i_own.at[:, 1 - core], i_core, is_s.at[0], is_r.at[0], other_core)
        send(io_own.at[:, 1 - core], io_core, is_s.at[1], is_r.at[1], other_core)
        send(ig_own, ig_core, is_s.at[2], is_r.at[2], other_core)

    def island_ring():
        got(i_core, is_r.at[0])
        got(io_core, is_r.at[1])
        got(ig_core, is_r.at[2])

        @pl.loop(0, 8)
        def _(n):
            i_core[n] = (i_core[n].astype(F32) + i_own[n, core].astype(F32)).astype(BF16)
            io_core[n] = (io_core[n].astype(F32) + io_own[n, core].astype(F32)).astype(BF16)

        ig_core[...] += ig_own[...]
        for step in range(1, 4):
            two = pl.ds(other_y(step) * 2, 2)
            send(i_core.at[two], i_ring.at[y], is_s.at[3 * step], is_r.at[3 * step], on_y(step))
            send(io_core.at[two], io_ring.at[y], is_s.at[3 * step + 1], is_r.at[3 * step + 1], on_y(step))
            send(ig_core, ig_ring.at[y], is_s.at[3 * step + 2], is_r.at[3 * step + 2], on_y(step))
        two = pl.ds(y * 2, 2)
        i_ring[y] = i_core[two]
        io_ring[y] = io_core[two]
        ig_ring[y] = ig_core[...]

    def island_far():
        for step in range(1, 4):
            source = other_y(4 - step)
            got(i_ring.at[source], is_r.at[3 * step])
            got(io_ring.at[source], is_r.at[3 * step + 1])
            got(ig_ring.at[source], is_r.at[3 * step + 2])
        i_ring[0] = (
            i_ring[0].astype(F32) + i_ring[1].astype(F32) + i_ring[2].astype(F32) + i_ring[3].astype(F32)
        ).astype(BF16)
        io_ring[0] = (
            io_ring[0].astype(F32) + io_ring[1].astype(F32) + io_ring[2].astype(F32) + io_ring[3].astype(F32)
        ).astype(BF16)
        ig_ring[0] = ig_ring[0] + ig_ring[1] + ig_ring[2] + ig_ring[3]
        send(i_ring.at[0, 1 - zh], i_far, is_s.at[12], is_r.at[12], other_far)
        send(io_ring.at[0, 1 - zh], io_far, is_s.at[13], is_r.at[13], other_far)
        send(ig_ring.at[0], ig_far, is_s.at[14], is_r.at[14], other_far)

    def island_sum():
        got(i_far, is_r.at[12])
        got(io_far, is_r.at[13])
        got(ig_far, is_r.at[14])
        totq_ref[...] = i_ring[0, zh].astype(F32) + i_far[...].astype(F32)
        toto_ref[...] = io_ring[0, zh].astype(F32) + io_far[...].astype(F32)
        total = ig_ring[0] + ig_far[...]
        for i in range(8):
            totg_ref[:, i * 256 : (i + 1) * 256] = total[i : i + 1, :]
        here = me // 2
        i_back[here, core] = nesterov(
            qglob_ref[...], qmom_ref[...], totq_ref[...] * (1.0 / islands)
        )[0].astype(BF16)
        io_back[here, core] = nesterov(
            oglob_ref[...], omom_ref[...], toto_ref[...] * (1.0 / islands)
        )[0].astype(BF16)
        send(i_back.at[here, core], i_back.at[here, core], is_s.at[15], is_r.at[15], other_far)
        send(io_back.at[here, core], io_back.at[here, core], is_s.at[16], is_r.at[16], other_far)
        store(totq_ref, totq_out)
        store(toto_ref, toto_out)
        store(totg_ref, totg_out)

    def back_ring():
        there = y * 2 + 1 - zh
        got(i_back.at[there, core], is_r.at[15])
        got(io_back.at[there, core], is_r.at[16])
        mine = i_back.at[pl.ds(y * 2, 2), core], io_back.at[pl.ds(y * 2, 2), core]
        for step in range(1, 4):
            for n in range(2):
                at = 17 + 2 * (step - 1) + n
                send(mine[n], mine[n], is_s.at[at], is_r.at[at], on_y(step))

    def back_core():
        for step in range(1, 4):
            source = pl.ds(other_y(4 - step) * 2, 2)
            got(i_back.at[source, core], is_r.at[17 + 2 * (step - 1)])
            got(io_back.at[source, core], is_r.at[18 + 2 * (step - 1)])
        send(i_back.at[:, core], i_back.at[:, core], is_s.at[23], is_r.at[23], other_core)
        send(io_back.at[:, core], io_back.at[:, core], is_s.at[24], is_r.at[24], other_core)

    def island_whole():
        got(i_back.at[:, 1 - core], is_r.at[23])
        got(io_back.at[:, 1 - core], is_r.at[24])
        for i in range(islands // 4):
            four = jnp.concatenate([i_back[2 * i + n // 2, n % 2] for n in range(4)], axis=0)
            wholeq_ref[:, i * 4 * qshare : (i + 1) * 4 * qshare] = four.astype(F32).T.astype(BF16)
        for i in range(islands):
            wholeo_ref[:, i * oshare : (i + 1) * oshare] = io_back[i // 2, i % 2]
        store(wholeq_ref, wholeq_out)
        store(wholeo_ref, wholeo_out)

    def normalise():
        @pl.loop(0, TOK // 128)
        def _(t):
            rows = rows_of(t, 128)
            wide = x_ref[rows, :].astype(F32)
            factor = lax.rsqrt(jnp.mean(wide * wide, axis=-1, keepdims=True) + NORM_EPS)
            fac[rows, :] = factor
            normed = (wide * factor * gain_ref[...]).astype(BF16)
            nrm[rows, :] = normed
            nrm_t[:, rows] = normed.astype(F32).T.astype(BF16)

    def turn(first, second, sign):
        cosine, sine = cos_ref[...], sin_ref[...] * sign
        return first * cosine - second * sine, first * sine + second * cosine

    def project(c):
        mixed = jnp.dot(nrm[...], wq[:, c * COLS : (c + 1) * COLS], preferred_element_type=F32)
        if c == VCHUNK:
            mixed = mixed.astype(BF16).astype(F32)
        mixed_t = mixed.T
        for n in range(COLS // HEAD_DIM):
            at = n * HEAD_DIM
            head = mixed_t[at : at + HEAD_DIM, :]
            if c != VCHUNK:
                first, second = turn(head[: HEAD_DIM // 2], head[HEAD_DIM // 2 :], 1.0)
                head = jnp.concatenate([first, second], axis=0)
            held = head.astype(BF16)
            if c < KCHUNK:
                held = (held.astype(F32) * HEAD_DIM ** (-0.5)).astype(BF16)
            qkv_t[c * COLS + at : c * COLS + at + HEAD_DIM, :] = held
            if c == KCHUNK:
                k_tok[n] = held.astype(F32).T.astype(BF16)
            if c == VCHUNK:
                v_tok[n] = held.astype(F32).T.astype(BF16)

    def project_back():
        @pl.loop(0, 8)
        def _(j):
            rows = rows_of(j, OROWS)
            datt_t[rows, :] = lax.dot_general(
                wo[rows, :], cot_ref[...], NT, preferred_element_type=F32
            ).astype(BF16)

    def attend(g):
        krows = slice(QW + g * HEAD_DIM, QW + (g + 1) * HEAD_DIM)
        vrows = slice(QW + (KV_HEADS + g) * HEAD_DIM, QW + (KV_HEADS + g + 1) * HEAD_DIM)
        dk_acc[...] = jnp.zeros_like(dk_acc)
        dv_acc[...] = jnp.zeros_like(dv_acc)

        @pl.loop(0, GROUP, unroll=2)
        def _(n):
            rows = rows_of(g * GROUP + n, HEAD_DIM)
            for q_at in range(0, TOK, QB):
                keys = q_at + QB
                queries = qkv_t[rows, q_at : q_at + QB]
                scores = jnp.dot(k_tok[g, :keys, :], queries, preferred_element_type=F32)
                key_at = lax.broadcasted_iota(jnp.int32, (QB, QB), 0)
                query_at = lax.broadcasted_iota(jnp.int32, (QB, QB), 1)
                masked = jnp.where(query_at >= key_at, scores[q_at:], -1e30)
                scores = jnp.concatenate([scores[:q_at], masked], axis=0) if q_at else masked
                top = jnp.max(scores, axis=0, keepdims=True)
                raised = jnp.exp(scores - top)
                soft = raised * (1.0 / jnp.sum(raised, axis=0, keepdims=True))
                weights = soft.astype(BF16)
                out = jnp.dot(qkv_t[vrows, :keys], weights, preferred_element_type=F32)
                att_t[rows, q_at : q_at + QB] = out.astype(BF16)
                dout = datt_t[rows, q_at : q_at + QB]
                dweights = jnp.dot(v_tok[g, :keys, :], dout, preferred_element_type=F32)
                dot_out = jnp.sum(out * dout.astype(F32), axis=0, keepdims=True)
                dscores = (soft * (dweights - dot_out)).astype(BF16)
                dqueries = jnp.dot(qkv_t[krows, :keys], dscores, preferred_element_type=F32)
                dqueries = (dqueries * HEAD_DIM ** (-0.5)).astype(BF16).astype(F32)
                half = HEAD_DIM // 2
                cosine, sine = cos_ref[:, q_at : q_at + QB], sin_ref[:, q_at : q_at + QB]
                first, second = dqueries[:half], dqueries[half:]
                dm_t[rows, q_at : q_at + QB] = jnp.concatenate(
                    [first * cosine + second * sine, second * cosine - first * sine], axis=0
                ).astype(BF16)
                dk_acc[:, :keys] += lax.dot_general(queries, dscores, NT, preferred_element_type=F32)
                dv_acc[:, :keys] += lax.dot_general(dout, weights, NT, preferred_element_type=F32)

        dkeys = dk_acc[...].astype(BF16).astype(F32)
        first, second = turn(dkeys[: HEAD_DIM // 2], dkeys[HEAD_DIM // 2 :], -1.0)
        dm_t[krows, :] = jnp.concatenate([first, second], axis=0).astype(BF16)
        dm_t[vrows, :] = dv_acc[...].astype(BF16)

    def gq_block(x_at, z_at, c):
        return gq.at[rows_of(x_at * 2 + z_at, QROWS), pl.ds(c * COLS, COLS)]

    def rq_at(n, c):
        return rq.at[n, :, pl.ds(c * COLS, COLS)]

    def grad_chunk(c):
        cols = slice(c * COLS, (c + 1) * COLS)

        @pl.loop(0, 8)
        def _(j):
            rows = rows_of(j, QROWS)
            gq[rows, cols] = lax.dot_general(
                nrm_t[rows, :], dm_t[cols, :], NT, preferred_element_type=F32
            ).astype(BF16)

        for n, (block, to) in enumerate((
            (gq_block(at_x(2), 0, c), left),
            (gq_block(at_x(2), 1, c), right),
            (gq_block(at_x(3), 1, c), left),
            (gq_block(at_x(1), 0, c), right),
        )):
            send(block, rq_at(n, c), rsq_s.at[c, n], rsq_r.at[c, n], to)
        dm[:, cols] = dm_t[cols, :].astype(F32).T.astype(BF16)

    def add_chunk(c):
        for n, (block, to) in enumerate(((gq_block(at_x(3), 0, c), left), (gq_block(at_x(1), 1, c), right))):
            got(rq_at(n, c), rsq_r.at[c, n])
            block[...] = (block[...].astype(F32) + rq_at(n, c)[...].astype(F32)).astype(BF16)
            send(block, rq_at(4 + n, c), rsq_s.at[c, 4 + n], rsq_r.at[c, 4 + n], to)

    def fold_chunk(c):
        for n in range(2, 6):
            got(rq_at(n, c), rsq_r.at[c, n])

        def whole(z_at, first, second):
            return (
                gq_block(a, z_at, c)[...].astype(F32)
                + rq.at[first, :, pl.ds(c * COLS, COLS)][...].astype(F32)
                + rq.at[second, :, pl.ds(c * COLS, COLS)][...].astype(F32)
            )

        block = gq_block(a, 1 - b, c)
        block[...] = whole(1 - b, 2 + b, 5 - b).astype(BF16)
        send(block, rq_at(6, c), rsq_s.at[c, 6], rsq_r.at[c, 6], across)
        block = gq_block(a, b, c)
        block[...] = whole(b, 3 - b, 4 + b).astype(BF16)

    def end_chunk(c):
        got(rq_at(6, c), rsq_r.at[c, 6])
        cols = pl.ds(c * COLS, COLS)
        sumq_ref[:, cols] = (gq_block(a, b, c)[...].astype(F32) + rq_at(6, c)[...].astype(F32)).astype(BF16)
        store(sumq_ref.at[:, cols], sumq_out.at[:, cols])

    def go_rows(x_at, z_at, half=None):
        start = (x_at * 2 + z_at) * OROWS
        if half is None:
            return go.at[pl.ds(pl.multiple_of(start, OROWS), OROWS)]
        return go.at[pl.ds(pl.multiple_of(start + half * HALF, HALF), HALF)]

    def grad_out(g):
        @pl.loop(0, 2)
        def _(z_at):
            rows = rows_of(2 * g + z_at, OROWS)
            go[rows, :] = jnp.dot(att_t[rows, :], cot_ref[...], preferred_element_type=F32).astype(BF16)

        send(go_rows(g, 1 - b), ro_z.at[g], rso_s.at[6 + g], rso_r.at[6 + g], across)

    def pair_out(step):
        x_at = at_x(step)
        got(ro_z.at[x_at], rso_r.at[6 + x_at])
        block = go_rows(x_at, b)
        block[...] = (block[...].astype(F32) + ro_z[x_at].astype(F32)).astype(BF16)

    def ring_out():
        pair_out(2)
        send(go_rows(at_x(2), b, 0), ro.at[0], rso_s.at[0], rso_r.at[0], left)
        send(go_rows(at_x(2), b, 1), ro.at[1], rso_s.at[1], rso_r.at[1], right)
        pair_out(3)
        send(go_rows(at_x(3), b, 1), ro.at[2], rso_s.at[2], rso_r.at[2], left)
        pair_out(1)
        send(go_rows(at_x(1), b, 0), ro.at[3], rso_s.at[3], rso_r.at[3], right)
        pair_out(0)

    def add_out():
        for n, (block, to) in enumerate(((go_rows(at_x(3), b, 0), left), (go_rows(at_x(1), b, 1), right))):
            got(ro.at[n], rso_r.at[n])
            block[...] = (block[...].astype(F32) + ro[n].astype(F32)).astype(BF16)
            send(block, ro.at[4 + n], rso_s.at[4 + n], rso_r.at[4 + n], to)

    def end_out():
        for n in range(2, 6):
            got(ro.at[n], rso_r.at[n])
        for half, (first, second) in enumerate(((3, 4), (2, 5))):
            sumo_ref[half * HALF : (half + 1) * HALF, :] = (
                go_rows(a, b, half)[...].astype(F32) + ro[first].astype(F32) + ro[second].astype(F32)
            ).astype(BF16)
        store(sumo_ref, sumo_out)

    def gain_grad():
        @pl.loop(0, 8)
        def _(j):
            dnormed = lax.dot_general(
                dm[...], wq[rows_of(j, QROWS), :], NT, preferred_element_type=F32
            ).astype(BF16).astype(F32)
            wide = x_ref[:, rows_of(j, QROWS)].astype(F32) * fac[...]
            g_rows[pl.ds(j, 1), :] = jnp.sum(dnormed * wide, axis=0, keepdims=True)

        @pl.loop(1, 8)
        def _(step):
            pltpu.make_async_remote_copy(
                src_ref=g_rows, dst_ref=g_recv.at[f], send_sem=gg_s.at[step], recv_sem=gg_r.at[step],
                device_id={"fsdp": lax.rem(f + step, 8)}, device_id_type=MESH,
            ).start()
        g_recv[f] = g_rows[...]

    def gain_sum():
        @pl.loop(1, 8)
        def _(step):
            got(g_recv.at[lax.rem(f - step + 8, 8)], gg_r.at[step])
        total = g_recv[0]
        for i in range(1, 8):
            total = total + g_recv[i]
        for i in range(8):
            sumg_ref[:, i * 256 : (i + 1) * 256] = total[i : i + 1, :]
        store(sumg_ref, sumg_out)

        @pl.loop(1, 8)
        def _(step):
            left_here(g_rows, gg_s.at[step])

    chunks[KCHUNK].own()
    out_paired.own()
    out_ringed.own()
    chunks[VCHUNK].own()
    chunks[0].own()
    chunks[KCHUNK].pair()
    for copy in loads[:6]:
        copy.wait()
    out_paired.pair()
    island_start()
    chunks[VCHUNK].pair()
    normalise()
    for copy in loads[6:]:
        copy.wait()
    out_ringed.onward()
    chunks[0].pair()
    island_ring()
    chunks[KCHUNK].onward()
    chunks[1].own()
    chunks[2].own()
    chunks[3].own()
    out_paired.onward()
    out_ringed.far()
    chunks[VCHUNK].onward()
    island_far()
    chunks[0].onward()
    chunks[KCHUNK].have()
    project(KCHUNK)
    chunks[1].pair()
    chunks[2].pair()
    island_sum()
    chunks[VCHUNK].have()
    project(VCHUNK)
    chunks[3].onward()
    back_ring()
    out_paired.have()
    out_ringed.have()
    project_back()
    chunks[0].have()
    project(0)
    back_core()
    attend(0)
    grad_chunk(0)
    chunks[1].onward()
    chunks[2].onward()
    chunks[3].far()
    grad_out(0)
    chunks[1].have()
    project(1)
    attend(1)
    grad_chunk(1)
    add_chunk(0)
    grad_out(1)
    chunks[2].have()
    project(2)
    attend(2)
    grad_chunk(2)
    add_chunk(1)
    grad_out(2)
    fold_chunk(0)
    chunks[3].have()
    project(3)
    attend(3)
    grad_chunk(3)
    grad_chunk(KCHUNK)
    grad_chunk(VCHUNK)
    add_chunk(2)
    grad_out(3)
    fold_chunk(1)
    add_chunk(3)
    fold_chunk(2)
    ring_out()
    add_chunk(KCHUNK)
    fold_chunk(3)
    add_chunk(VCHUNK)
    add_out()
    gain_grad()
    end_chunk(0)
    end_chunk(1)
    fold_chunk(KCHUNK)
    island_whole()
    fold_chunk(VCHUNK)
    end_chunk(2)
    end_chunk(3)
    end_out()
    end_chunk(KCHUNK)
    gain_sum()
    end_chunk(VCHUNK)
    for copy in stores:
        copy.wait()
    for src, s_sem in sent:
        left_here(src, s_sem)


def grads(islands, x, cot, gain, wq, wo, qglob, qmom, oglob, omom):
    qshare, oshare = QKV // islands, D // islands
    cosine, sine = rope_tables()
    hbm = pl.BlockSpec(memory_space=pl.ANY)
    dma = pltpu.SemaphoreType.DMA
    operands = (x, cot, gain, wq, wo, jnp.asarray(cosine), jnp.asarray(sine), qglob, qmom, oglob, omom)
    results = [
        jax.ShapeDtypeStruct((QROWS, QKV), BF16),
        jax.ShapeDtypeStruct((OROWS, D), BF16),
        jax.ShapeDtypeStruct((1, D), F32),
        jax.ShapeDtypeStruct((qshare, QROWS), F32),
        jax.ShapeDtypeStruct((OROWS, oshare), F32),
        jax.ShapeDtypeStruct((1, D), F32),
        jax.ShapeDtypeStruct((QROWS, QKV), BF16),
        jax.ShapeDtypeStruct((OROWS, D), BF16),
    ]
    return pl.pallas_call(
        functools.partial(grads_kernel, islands),
        out_shape=results,
        in_specs=[hbm] * 11,
        out_specs=[hbm] * 8,
        scratch_shapes=[
            *(pltpu.VMEM(operands[n].shape, operands[n].dtype) for n in (0, 1, 2, 5, 6, 7, 8, 9, 10)),
            *(pltpu.VMEM(r.shape, r.dtype) for r in results),
            pltpu.VMEM((D, QKV), BF16),
            pltpu.VMEM((QW, D), BF16),
            pltpu.VMEM((TOK, D), BF16),
            pltpu.VMEM((D, TOK), BF16),
            pltpu.VMEM((TOK, 1), F32),
            pltpu.VMEM((QKV, TOK), BF16),
            pltpu.VMEM((KV_HEADS, TOK, HEAD_DIM), BF16),
            pltpu.VMEM((KV_HEADS, TOK, HEAD_DIM), BF16),
            pltpu.VMEM((QW, TOK), BF16),
            pltpu.VMEM((QW, TOK), BF16),
            pltpu.VMEM((QKV, TOK), BF16),
            pltpu.VMEM((TOK, QKV), BF16),
            pltpu.VMEM((HEAD_DIM, TOK), F32),
            pltpu.VMEM((HEAD_DIM, TOK), F32),
            pltpu.VMEM((D, QKV), BF16),
            pltpu.VMEM((QW, D), BF16),
            pltpu.VMEM((7, QROWS, QKV), BF16),
            pltpu.VMEM((6, HALF, D), BF16),
            pltpu.VMEM((4, OROWS, D), BF16),
            pltpu.VMEM((8, 256), F32),
            pltpu.VMEM((8, 8, 256), F32),
            pltpu.VMEM((8, 2, qshare, QROWS), BF16),
            pltpu.VMEM((8, 2, OROWS, oshare), BF16),
            pltpu.VMEM((8, qshare, QROWS), BF16),
            pltpu.VMEM((8, OROWS, oshare), BF16),
            pltpu.VMEM((8, 256), F32),
            pltpu.VMEM((4, 2, qshare, QROWS), BF16),
            pltpu.VMEM((4, 2, OROWS, oshare), BF16),
            pltpu.VMEM((4, 8, 256), F32),
            pltpu.VMEM((qshare, QROWS), BF16),
            pltpu.VMEM((OROWS, oshare), BF16),
            pltpu.VMEM((8, 256), F32),
            pltpu.VMEM((8, 256), F32),
            pltpu.VMEM((8, 2, qshare, QROWS), BF16),
            pltpu.VMEM((8, 2, OROWS, oshare), BF16),
            dma((11,)),
            dma((13,)),
            dma((CHUNKS, 7)), dma((CHUNKS, 7)),
            dma((2, 9)), dma((2, 9)),
            dma((CHUNKS, 7)), dma((CHUNKS, 7)),
            dma((10,)), dma((10,)),
            dma((8,)), dma((8,)),
            dma((25,)), dma((25,)),
        ],
        compiler_params=pltpu.CompilerParams(
            collective_id=0, has_side_effects=True, vmem_limit_bytes=63 * 2**20
        ),
        name="grads",
    )(*operands)


PARTS = 4


def update_kernel(islands, *refs):
    (
        gain_ref, wq_in, wo_in, gf_ref, gs_ref, qf_in, qs_in, of_in, os_in,
        gg_ref, gm_ref, qg_ref, qm_ref, og_ref, om_ref,
        sumq_in, sumo_in, sumg_ref, totq_ref, toto_ref, totg_ref, wholeq_in, wholeo_in,
        gain_o, wq_out, wo_out, gf_o, gs_o, qf_out, qs_out, of_out, os_out,
        gg_o, gm_o, qg_o, qm_o, og_o, om_o,
        *scratch, in_sem, out_sem,
    ) = refs
    sources = (wq_in, sumq_in, qf_in, qs_in, wholeq_in, wo_in, sumo_in, of_in, os_in, wholeo_in)
    targets = (wq_out, qf_out, qs_out, wo_out, of_out, os_out)
    held, made = scratch[: len(sources)], scratch[len(sources) :]

    def part(ref, i):
        size = ref.shape[0] // PARTS
        return ref.at[pl.ds(i * size, size)]

    loads = [
        [pltpu.make_async_copy(part(src, i), part(dst, i), in_sem.at[i, n]) for n, (src, dst) in enumerate(zip(sources, held))]
        for i in range(PARTS)
    ]
    for row in loads:
        for copy in row:
            copy.start()
    scale = 1.0 / islands
    stepped, first, second = adamw(gain_ref[...], sumg_ref[...], gf_ref[...], gs_ref[...], 0.0)
    outer, momentum = nesterov(gg_ref[...], gm_ref[...], totg_ref[...] * scale)
    gain_o[...] = MIXING * stepped + (1.0 - MIXING) * outer
    gf_o[...] = first
    gs_o[...] = second
    gg_o[...] = outer
    gm_o[...] = momentum
    qg_o[...], qm_o[...] = nesterov(qg_ref[...], qm_ref[...], totq_ref[...] * scale)
    og_o[...], om_o[...] = nesterov(og_ref[...], om_ref[...], toto_ref[...] * scale)
    stores = []
    for i in range(PARTS):
        for copy in loads[i]:
            copy.wait()
        for which in range(2):
            w, s, m1, m2, whole = (part(ref, i) for ref in held[5 * which : 5 * which + 5])
            outs = [part(ref, i) for ref in made[3 * which : 3 * which + 3]]
            stepped, first, second = adamw(w[...], s[...].astype(F32), m1[...], m2[...], WEIGHT_DECAY)
            outs[0][...] = (MIXING * stepped + (1.0 - MIXING) * whole[...].astype(F32)).astype(BF16)
            outs[1][...] = first
            outs[2][...] = second
            for n in range(3):
                copy = pltpu.make_async_copy(
                    outs[n], part(targets[3 * which + n], i), out_sem.at[i, 3 * which + n]
                )
                copy.start()
                stores.append(copy)
    for copy in stores:
        copy.wait()


def update(islands, state, sums):
    def spec(array):
        big = array.shape in ((QROWS, QKV), (OROWS, D))
        return pl.BlockSpec(memory_space=pl.ANY if big else pltpu.VMEM)

    def room(*arrays):
        return [pltpu.VMEM(v.shape, v.dtype) for v in arrays]

    return pl.pallas_call(
        functools.partial(update_kernel, islands),
        out_shape=[jax.ShapeDtypeStruct(o.shape, o.dtype) for o in state],
        in_specs=[spec(v) for v in (*state, *sums)],
        out_specs=[spec(o) for o in state],
        scratch_shapes=[
            *room(state[1], sums[0], state[5], state[6], sums[6], state[2], sums[1], state[7], state[8], sums[7]),
            *room(state[1], state[5], state[6], state[2], state[7], state[8]),
            pltpu.SemaphoreType.DMA((PARTS, 10)),
            pltpu.SemaphoreType.DMA((PARTS, 6)),
        ],
        compiler_params=pltpu.CompilerParams(vmem_limit_bytes=60 * 2**20),
        name="update",
    )(*state, *sums)


def shards(
    tokens, cotangent, norm_gain, qkv_weight, out_weight, gain_first, gain_second,
    qkv_first, qkv_second, out_first, out_second,
    gain_global, gain_momentum, qkv_global, qkv_momentum, out_global, out_momentum,
):
    islands = lax.axis_size("island")
    wq, wo = qkv_weight[0], out_weight[0]
    qkv_global, qkv_momentum = qkv_global.T, qkv_momentum.T
    sums = grads(
        islands, tokens, cotangent, norm_gain, wq, wo, qkv_global, qkv_momentum, out_global, out_momentum
    )
    state = (
        norm_gain, wq, wo, gain_first, gain_second, qkv_first[0], qkv_second[0], out_first[0], out_second[0],
        gain_global[None], gain_momentum[None], qkv_global, qkv_momentum, out_global, out_momentum,
    )
    (
        gain_next, wq_next, wo_next, gf, gs, qf, qs, of, os_, gg, gm, qg, qm, og, om
    ) = update(islands, state, sums)
    return (
        gain_next, wq_next[None], wo_next[None], gf, gs, qf[None], qs[None], of[None], os_[None],
        gg[0], gm[0], qg.T, qm.T, og, om,
    )


def solution(mesh):
    placed = (
        P(("island", "fsdp"), None),
        P(("island", "fsdp"), None),
        P("island", None),
        P("island", "fsdp", None),
        P("island", "fsdp", None),
        P("island", None),
        P("island", None),
        P("island", "fsdp", None),
        P("island", "fsdp", None),
        P("island", "fsdp", None),
        P("island", "fsdp", None),
        P(),
        P(),
        P("fsdp", "island"),
        P("fsdp", "island"),
        P("fsdp", "island"),
        P("fsdp", "island"),
    )
    return jax.shard_map(
        shards,
        mesh=mesh,
        in_specs=placed,
        out_specs=(
            P("island", None),
            P("island", "fsdp", None),
            P("island", "fsdp", None),
            P("island", None),
            P("island", None),
            P("island", "fsdp", None),
            P("island", "fsdp", None),
            P("island", "fsdp", None),
            P("island", "fsdp", None),
            P(),
            P(),
            P("fsdp", "island"),
            P("fsdp", "island"),
            P("fsdp", "island"),
            P("fsdp", "island"),
        ),
        check_vma=False,
    )
```

time: 235 us -> 179 us (0.76)
  Pallas kernels: 209 us -> 177 us
  local copies, waits for them, and re-layouts: 24.2 us -> 0 us
    pallas_call x2, Pallas kernels: 209 us -> 177 us  [the longest x1 168 us: grads(): pl.pallas_call(functools.partial(grads_kernel, islands), out_shape=result...]
    unnamed x50 -> x0, local copies, waits for them, and re-layouts: 24.2 us -> none
where the time goes in v2:
time: 179 us; the launch traced here: 178 us
  Pallas kernels  177 us (99%)
    pallas_call x1, Pallas kernels, grads(): pl.pallas_call(functools.partial(grads_kernel, islands), out_shape=result...  168 us
    pallas_call x1, Pallas kernels, update(): pl.pallas_call(functools.partial(update_kernel, islands), out_shape=[jax....  9.52 us

profile of v2, /device:TPU:64, one launch (start us, length us, event | category | flops | bytes accessed | tf_op | source)
XLA Modules:
  0.0 178.2 jit_solution(4540520577241378940)
XLA Ops:
  0.6 167.8 %grads.1 = (bf16[256,1536]{1,0:T(8,128)(2,1)}, bf16[128,2048]{1,0:T(8,128)(2,1)}, f32[1,2048]{1,0:T(1,128)}, f32[96,256]{1,0:T(8,128)}, f32[128,128]{1,0:T(8,128...) custom-call(bf16[512,2048]{1,0:T(8,128)(2,1)} %x_in.1, bf16[512,2048]{1,0:T(8,128)(2,1)} %cot_in.1, ...), custom_call_target="tpu_custom_call" | custom-call | tf_op jit(solution)/shard_map/grads/pallas_call | solution.py:671
  168.5 9.5 %update.1 = (f32[1,2048]{1,0:T(1,128)}, bf16[256,1536]{1,0:T(8,128)(2,1)}, bf16[128,2048]{1,0:T(8,128)(2,1)}, f32[1,2048]{1,0:T(1,128)}, f32[1,2048]{1,0:T(1,128...) custom-call(f32[1,2048]{1,0:T(1,128)} %refs_0_.1, ...), custom_call_target="tpu_custom_call" | custom-call | tf_op jit(solution)/shard_map/update/pallas_call | solution.py:796

commit v3 on v2

--- a/solution.py
+++ b/solution.py
@@ -36,11 +36,11 @@
 QROWS = 256
 OROWS = 128
 HALF = OROWS // 2
-OPAIRED = 512
+OPAIRED = 896
 COLS = 256
 CHUNKS = QKV // COLS
 KCHUNK, VCHUNK = QW // COLS, QW // COLS + 1
-QB = 256
+QB = 512
 NT = (((1,), (1,)), ((), ()))
 
 
@@ -377,9 +377,9 @@
                 v_tok[n] = held.astype(F32).T.astype(BF16)
 
     def project_back():
-        @pl.loop(0, 8)
+        @pl.loop(0, 2)
         def _(j):
-            rows = rows_of(j, OROWS)
+            rows = rows_of(j, QW // 2)
             datt_t[rows, :] = lax.dot_general(
                 wo[rows, :], cot_ref[...], NT, preferred_element_type=F32
             ).astype(BF16)
@@ -436,12 +436,12 @@
     def grad_chunk(c):
         cols = slice(c * COLS, (c + 1) * COLS)
 
-        @pl.loop(0, 8)
+        dm[:, cols] = dm_t[cols, :].astype(F32).T.astype(BF16)
+
+        @pl.loop(0, 2)
         def _(j):
-            rows = rows_of(j, QROWS)
-            gq[rows, cols] = lax.dot_general(
-                nrm_t[rows, :], dm_t[cols, :], NT, preferred_element_type=F32
-            ).astype(BF16)
+            rows = rows_of(j, D // 2)
+            gq[rows, cols] = jnp.dot(nrm_t[rows, :], dm[:, cols], preferred_element_type=F32).astype(BF16)
 
         for n, (block, to) in enumerate((
             (gq_block(at_x(2), 0, c), left),
@@ -450,7 +450,6 @@
             (gq_block(at_x(1), 0, c), right),
         )):
             send(block, rq_at(n, c), rsq_s.at[c, n], rsq_r.at[c, n], to)
-        dm[:, cols] = dm_t[cols, :].astype(F32).T.astype(BF16)
 
     def add_chunk(c):
         for n, (block, to) in enumerate(((gq_block(at_x(3), 0, c), left), (gq_block(at_x(1), 1, c), right))):
@@ -488,10 +487,12 @@
         return go.at[pl.ds(pl.multiple_of(start + half * HALF, HALF), HALF)]
 
     def grad_out(g):
+        rows = slice(2 * g * OROWS, 2 * (g + 1) * OROWS)
+
         @pl.loop(0, 2)
-        def _(z_at):
-            rows = rows_of(2 * g + z_at, OROWS)
-            go[rows, :] = jnp.dot(att_t[rows, :], cot_ref[...], preferred_element_type=F32).astype(BF16)
+        def _(n):
+            cols = rows_of(n, D // 2)
+            go[rows, cols] = jnp.dot(att_t[rows, :], cot_ref[:, cols], preferred_element_type=F32).astype(BF16)
 
         send(go_rows(g, 1 - b), ro_z.at[g], rso_s.at[6 + g], rso_r.at[6 + g], across)
 
@@ -558,41 +559,41 @@
         def _(step):
             left_here(g_rows, gg_s.at[step])
 
+    out_ringed.own()
     chunks[KCHUNK].own()
     out_paired.own()
-    out_ringed.own()
+    for copy in loads[:6]:
+        copy.wait()
+    island_start()
+    normalise()
     chunks[VCHUNK].own()
     chunks[0].own()
     chunks[KCHUNK].pair()
-    for copy in loads[:6]:
-        copy.wait()
     out_paired.pair()
-    island_start()
-    chunks[VCHUNK].pair()
-    normalise()
     for copy in loads[6:]:
         copy.wait()
     out_ringed.onward()
-    chunks[0].pair()
     island_ring()
     chunks[KCHUNK].onward()
+    chunks[VCHUNK].pair()
+    chunks[0].pair()
     chunks[1].own()
     chunks[2].own()
     chunks[3].own()
     out_paired.onward()
     out_ringed.far()
+    island_far()
     chunks[VCHUNK].onward()
-    island_far()
     chunks[0].onward()
     chunks[KCHUNK].have()
     project(KCHUNK)
+    island_sum()
     chunks[1].pair()
     chunks[2].pair()
-    island_sum()
     chunks[VCHUNK].have()
     project(VCHUNK)
+    back_ring()
     chunks[3].onward()
-    back_ring()
     out_paired.have()
     out_ringed.have()
     project_back()
@@ -727,7 +728,7 @@
     )(*operands)
 
 
-PARTS = 4
+PARTS = 2
 
 
 def update_kernel(islands, *refs):

time: 179 us -> 171 us (0.955); the launches traced: 178 us -> 168 us
  Pallas kernels: 177 us -> 168 us
    pallas_call x1, Pallas kernels: 168 us -> 159 us  [grads(): pl.pallas_call(functools.partial(grads_kernel, islands), out_shape=result...]
where the time goes in v3:
time: 171 us; the launch traced here: 168 us
  Pallas kernels  168 us (98%)
    pallas_call x1, Pallas kernels, grads(): pl.pallas_call(functools.partial(grads_kernel, islands), out_shape=result...  159 us
    pallas_call x1, Pallas kernels, update(): pl.pallas_call(functools.partial(update_kernel, islands), out_shape=[jax....  8.28 us

profile of v3, /device:TPU:64, one launch (start us, length us, event | category | flops | bytes accessed | tf_op | source)
XLA Modules:
  0.0 168.4 jit_solution(14878312361376763999)
XLA Ops:
  0.6 159.3 %grads.1 = (bf16[256,1536]{1,0:T(8,128)(2,1)}, bf16[128,2048]{1,0:T(8,128)(2,1)}, f32[1,2048]{1,0:T(1,128)}, f32[96,256]{1,0:T(8,128)}, f32[128,128]{1,0:T(8,128...) custom-call(bf16[512,2048]{1,0:T(8,128)(2,1)} %x_in.1, bf16[512,2048]{1,0:T(8,128)(2,1)} %cot_in.1, ...), custom_call_target="tpu_custom_call" | custom-call | tf_op jit(solution)/shard_map/grads/pallas_call | solution.py:672
  159.9 8.3 %update.1 = (f32[1,2048]{1,0:T(1,128)}, bf16[256,1536]{1,0:T(8,128)(2,1)}, bf16[128,2048]{1,0:T(8,128)(2,1)}, f32[1,2048]{1,0:T(1,128)}, f32[1,2048]{1,0:T(1,128...) custom-call(f32[1,2048]{1,0:T(1,128)} %refs_0_.1, ...), custom_call_target="tpu_custom_call" | custom-call | tf_op jit(solution)/shard_map/update/pallas_call | solution.py:797

commit v4 on v3

--- a/solution.py
+++ b/solution.py
@@ -390,7 +390,7 @@
         dk_acc[...] = jnp.zeros_like(dk_acc)
         dv_acc[...] = jnp.zeros_like(dv_acc)
 
-        @pl.loop(0, GROUP, unroll=2)
+        @pl.loop(0, GROUP, unroll=4)
         def _(n):
             rows = rows_of(g * GROUP + n, HEAD_DIM)
             for q_at in range(0, TOK, QB):
@@ -728,20 +728,30 @@
     )(*operands)
 
 
+SMALL = (0, 3, 4, 9, 10, 11, 12, 13, 14)
 PARTS = 2
 
 
 def update_kernel(islands, *refs):
     (
-        gain_ref, wq_in, wo_in, gf_ref, gs_ref, qf_in, qs_in, of_in, os_in,
-        gg_ref, gm_ref, qg_ref, qm_ref, og_ref, om_ref,
-        sumq_in, sumo_in, sumg_ref, totq_ref, toto_ref, totg_ref, wholeq_in, wholeo_in,
-        gain_o, wq_out, wo_out, gf_o, gs_o, qf_out, qs_out, of_out, os_out,
-        gg_o, gm_o, qg_o, qm_o, og_o, om_o,
-        *scratch, in_sem, out_sem,
+        gain_in, wq_in, wo_in, gf_in, gs_in, qf_in, qs_in, of_in, os_in,
+        gg_in, gm_in, qg_in, qm_in, og_in, om_in,
+        sumq_in, sumo_in, sumg_in, totq_in, toto_in, totg_in, wholeq_in, wholeo_in,
+        gain_out, wq_out, wo_out, gf_out, gs_out, qf_out, qs_out, of_out, os_out,
+        gg_out, gm_out, qg_out, qm_out, og_out, om_out,
+        *scratch, in_sem, out_sem, small_in_sem, small_out_sem,
     ) = refs
     sources = (wq_in, sumq_in, qf_in, qs_in, wholeq_in, wo_in, sumo_in, of_in, os_in, wholeo_in)
     targets = (wq_out, qf_out, qs_out, wo_out, of_out, os_out)
+    small_sources = (
+        gain_in, gf_in, gs_in, gg_in, gm_in, qg_in, qm_in, og_in, om_in, sumg_in, totq_in, toto_in, totg_in
+    )
+    small_targets = (gain_out, gf_out, gs_out, gg_out, gm_out, qg_out, qm_out, og_out, om_out)
+    scratch, small_made = scratch[:-9], scratch[-9:]
+    scratch, small_held = scratch[:-13], scratch[-13:]
+    gain_ref, gf_ref, gs_ref, gg_ref, gm_ref, qg_ref, qm_ref, og_ref, om_ref = small_held[:9]
+    sumg_ref, totq_ref, toto_ref, totg_ref = small_held[9:]
+    gain_o, gf_o, gs_o, gg_o, gm_o, qg_o, qm_o, og_o, om_o = small_made
     held, made = scratch[: len(sources)], scratch[len(sources) :]
 
     def part(ref, i):
@@ -755,6 +765,13 @@
     for row in loads:
         for copy in row:
             copy.start()
+    small_loads = [
+        pltpu.make_async_copy(src, dst, small_in_sem.at[n]) for n, (src, dst) in enumerate(zip(small_sources, small_held))
+    ]
+    for copy in small_loads:
+        copy.start()
+    for copy in small_loads:
+        copy.wait()
     scale = 1.0 / islands
     stepped, first, second = adamw(gain_ref[...], sumg_ref[...], gf_ref[...], gs_ref[...], 0.0)
     outer, momentum = nesterov(gg_ref[...], gm_ref[...], totg_ref[...] * scale)
@@ -765,7 +782,11 @@
     gm_o[...] = momentum
     qg_o[...], qm_o[...] = nesterov(qg_ref[...], qm_ref[...], totq_ref[...] * scale)
     og_o[...], om_o[...] = nesterov(og_ref[...], om_ref[...], toto_ref[...] * scale)
-    stores = []
+    stores = [
+        pltpu.make_async_copy(src, dst, small_out_sem.at[n]) for n, (src, dst) in enumerate(zip(small_made, small_targets))
+    ]
+    for copy in stores:
+        copy.start()
     for i in range(PARTS):
         for copy in loads[i]:
             copy.wait()
@@ -787,9 +808,7 @@
 
 
 def update(islands, state, sums):
-    def spec(array):
-        big = array.shape in ((QROWS, QKV), (OROWS, D))
-        return pl.BlockSpec(memory_space=pl.ANY if big else pltpu.VMEM)
+    hbm = pl.BlockSpec(memory_space=pl.ANY)
 
     def room(*arrays):
         return [pltpu.VMEM(v.shape, v.dtype) for v in arrays]
@@ -797,13 +816,17 @@
     return pl.pallas_call(
         functools.partial(update_kernel, islands),
         out_shape=[jax.ShapeDtypeStruct(o.shape, o.dtype) for o in state],
-        in_specs=[spec(v) for v in (*state, *sums)],
-        out_specs=[spec(o) for o in state],
+        in_specs=[hbm] * (len(state) + len(sums)),
+        out_specs=[hbm] * len(state),
         scratch_shapes=[
             *room(state[1], sums[0], state[5], state[6], sums[6], state[2], sums[1], state[7], state[8], sums[7]),
             *room(state[1], state[5], state[6], state[2], state[7], state[8]),
+            *room(*(state[n] for n in SMALL), sums[2], sums[3], sums[4], sums[5]),
+            *room(*(state[n] for n in SMALL)),
             pltpu.SemaphoreType.DMA((PARTS, 10)),
             pltpu.SemaphoreType.DMA((PARTS, 6)),
+            pltpu.SemaphoreType.DMA((13,)),
+            pltpu.SemaphoreType.DMA((9,)),
         ],
         compiler_params=pltpu.CompilerParams(vmem_limit_bytes=60 * 2**20),
         name="update",

time: 171 us -> 170 us (level)
  no operation moved by 1% of the time
where the time goes in v4:
time: 170 us; the launch traced here: 168 us
  Pallas kernels  167 us (98%)
    pallas_call x1, Pallas kernels, grads(): pl.pallas_call(functools.partial(grads_kernel, islands), out_shape=result...  159 us
    pallas_call x1, Pallas kernels, update(): pl.pallas_call(functools.partial(update_kernel, islands), out_shape=[jax....  7.96 us

profile of v4, /device:TPU:64, one launch (start us, length us, event | category | flops | bytes accessed | tf_op | source)
XLA Modules:
  0.0 167.7 jit_solution(16562220444309837980)
XLA Ops:
  0.6 158.9 %grads.1 = (bf16[256,1536]{1,0:T(8,128)(2,1)}, bf16[128,2048]{1,0:T(8,128)(2,1)}, f32[1,2048]{1,0:T(1,128)}, f32[96,256]{1,0:T(8,128)}, f32[128,128]{1,0:T(8,128...) custom-call(bf16[512,2048]{1,0:T(8,128)(2,1)} %x_in.1, bf16[512,2048]{1,0:T(8,128)(2,1)} %cot_in.1, ...), custom_call_target="tpu_custom_call" | custom-call | tf_op jit(solution)/shard_map/grads/pallas_call | solution.py:672
  159.5 8.0 %update.1 = (f32[1,2048]{1,0:T(1,128)}, bf16[256,1536]{1,0:T(8,128)(2,1)}, bf16[128,2048]{1,0:T(8,128)(2,1)}, f32[1,2048]{1,0:T(1,128)}, f32[1,2048]{1,0:T(1,128...) custom-call(f32[1,2048]{1,0:T(1,128)} %refs_0_.1, ...), custom_call_target="tpu_custom_call" | custom-call | tf_op jit(solution)/shard_map/update/pallas_call | solution.py:816
